TPU v7x, 256 devices: a whole 4x4x8 slice. The times are simulated.
256 devices in a mesh: row: 8 (over y, core), col: 32 (over z, x).
Axes of the slice: x: 4, y: 4, z: 8, core: 2. Of those that a mesh axis runs over, the one named last changes fastest.
Arguments:
- matrix: float32 [16384, 16384], P('row', 'col'), as said below
Outputs:
- updated: float32 [16384, 16384], P('row', 'col')
- reflectors: float32 [1, 16384, 256], P(None, ('row', 'col'))
- products: float32 [1, 16384, 256], P(None, ('row', 'col'))
Inputs may be any that keep to these rules, and one draw needn't show every extreme that they name: `matrix`: symmetric.
All inputs are finite; a program needn't handle non-finite values.
Results may differ from a plain program's by a relative error of at most 0.0003.
Values sent between devices are 32-bit elements; how exact they have to be, the bound alone decides.
No kernel may reach another device: no remote copies, remote signals or barrier semaphores. Data moves between devices by JAX's collectives and lax.ppermute only.
A program may use at most 64 MiB of HBM per device.

v0:
```python
import jax
import jax.numpy as jnp
from jax import lax
from jax.experimental import pallas as pl
from jax.experimental.pallas import tpu as pltpu
from jax.sharding import PartitionSpec as P

HI = lax.Precision.HIGHEST
NB = 256
BK = 64
STEPS = NB // BK
LOOK = 8


def dot(a, b, ca=1, cb=0):
    return lax.dot_general(a, b, (((ca,), (cb,)), ((), ())), precision=HI, preferred_element_type=jnp.float32)


def lanes_of(chunk, k):
    return jnp.broadcast_to(chunk[:, k : k + 1], chunk.shape)


def leaf_start(block, below):
    eye = jnp.eye(BK, dtype=jnp.float32)
    top = jnp.concatenate([block, eye], axis=1)
    rows = [top[8 * i : 8 * i + 8] for i in range(BK // 8)]
    if below:
        low = jnp.concatenate([eye, jnp.zeros((BK, BK), jnp.float32)], axis=1)
        rows += [low[8 * i : 8 * i + 8] for i in range(BK // 8)]
    return {"rows": rows, "below": below, "recip": [], "sign": [], "pivot": []}


def leaf_group(state, first, look, signed):
    rows = state["rows"]
    half = BK // 8
    lane = lax.broadcasted_iota(jnp.int32, (1, 2 * BK), 1)
    sub = lax.broadcasted_iota(jnp.int32, (8, 2 * BK), 0)
    active = list(range(first // 8, half))
    if state["below"]:
        active += list(range(half, half + (first + look - 1) // 8 + 1))
    cols = [{i: lanes_of(rows[i], first + j) for i in active} for j in range(look)]
    for j in range(look):
        k = first + j
        own, off = k // 8, k % 8
        pivot = cols[j][own][off : off + 1]
        if signed:
            sign = jnp.where(pivot >= 0, 1.0, -1.0).astype(jnp.float32)
            pivot = pivot + sign
            state["sign"].append(sign)
        recip = 1.0 / pivot
        state["recip"].append(recip)
        state["pivot"].append(pivot)
        scaled = jnp.where(lane > k, rows[own][off : off + 1] * recip, 0.0)
        ahead = [cols[jj][own][off : off + 1] * recip for jj in range(j + 1, look)]
        for i in active:
            if i < half and i == own:
                if off == 7:
                    continue
                mult = jnp.where(sub > off, cols[j][i], 0.0)
            else:
                mult = cols[j][i]
            rows[i] = rows[i] - mult * scaled
            for n, jj in enumerate(range(j + 1, look)):
                cols[jj][i] = cols[jj][i] - mult * ahead[n]


def pick(rows):
    lane = lax.broadcasted_iota(jnp.int32, (1, 2 * BK), 1)
    out = jnp.zeros((1, 2 * BK), jnp.float32)
    for k, row in enumerate(rows):
        out = jnp.where(lane == k, row, out)
    return out[:, :BK]


def factor_step(p, refs):
    h_ref, l_ref, u_ref, li_ref, ui_ref, s_ref, y_ref = refs
    chol = lu = None
    if p < STEPS:
        chol = leaf_start(h_ref[p * BK : (p + 1) * BK, p * BK : (p + 1) * BK], False)
    if p > 0:
        lu = leaf_start(y_ref[(p - 1) * BK : p * BK, :], True)
    for first in range(0, BK, LOOK):
        if chol is not None:
            leaf_group(chol, first, LOOK, False)
        if lu is not None:
            leaf_group(lu, first, LOOK, True)
    tri_r = lax.broadcasted_iota(jnp.int32, (BK, BK), 0)
    tri_c = lax.broadcasted_iota(jnp.int32, (BK, BK), 1)
    half = BK // 8
    if chol is not None:
        inv_low = jnp.concatenate(chol["rows"], axis=0)[:, BK:]
        recip = pick(chol["recip"])
        scale = jnp.sqrt(recip)
        panel = dot(h_ref[:, p * BK : (p + 1) * BK], inv_low, 1, 1) * scale
        h_ref[:, p * BK : (p + 1) * BK] = panel
        if p + 1 < STEPS:
            after = panel[(p + 1) * BK : NB]
            h_ref[:, (p + 1) * BK :] = h_ref[:, (p + 1) * BK :] - dot(panel, after, 1, 1)
    if lu is not None:
        q0, q1 = (p - 1) * BK, p * BK
        full = jnp.concatenate(lu["rows"][:half], axis=0)
        low_inv = full[:, BK:]
        recip = pick(lu["recip"])
        pivot = pick(lu["pivot"])
        s_ref[:, q0:q1] = pick(lu["sign"])
        main = full[:, :BK]
        l_diag = jnp.where(tri_r > tri_c, main * recip, jnp.where(tri_r == tri_c, 1.0, 0.0))
        u_diag = jnp.where(tri_r < tri_c, main, jnp.where(tri_r == tri_c, pivot, 0.0))
        low = jnp.concatenate(lu["rows"][half:], axis=0)[:, :BK]
        u_inv = jnp.where(tri_r <= tri_c, low * recip, 0.0)
        l_ref[q0:q1, q0:q1] = l_diag
        u_ref[q0:q1, q0:q1] = u_diag
        li_ref[q0:q1, q0:q1] = low_inv
        ui_ref[q0:q1, q0:q1] = u_inv
        if p < STEPS:
            l_ref[q1:, q0:q1] = dot(y_ref[q1:, :], u_inv)
        if p > 1:
            li_ref[q0:q1, :q0] = -dot(low_inv, dot(l_ref[q0:q1, :q0], li_ref[:q0, :q0]))
            ui_ref[:q0, q0:q1] = -dot(ui_ref[:q0, :q0], dot(u_ref[:q0, q0:q1], u_inv))
    if p < STEPS:
        q1 = p * BK
        col = h_ref[NB : 2 * NB, p * BK : (p + 1) * BK]
        if p > 0:
            upper = dot(li_ref[:q1, :q1], col[:q1])
            u_ref[:q1, q1 : q1 + BK] = upper
            y_ref[q1:, :] = col[q1:] - dot(l_ref[q1:, :q1], upper)
        else:
            y_ref[...] = col


def factor_all(gram, top):
    def kernel(g_ref, c_ref, l_out, u_out, li_out, m_out, ri_out, s_out, h, y, ui):
        h[:NB] = g_ref[...]
        h[NB : 2 * NB] = c_ref[...]
        r = lax.broadcasted_iota(jnp.int32, (NB, NB), 0)
        c = lax.broadcasted_iota(jnp.int32, (NB, NB), 1)
        h[2 * NB :] = jnp.where(r == c, 1.0, 0.0).astype(jnp.float32)
        for ref in (l_out, u_out, li_out, ui):
            ref[...] = jnp.zeros((NB, NB), jnp.float32)
        for p in range(STEPS + 1):
            factor_step(p, (h, l_out, u_out, li_out, ui, s_out, y))
        r_inv = h[2 * NB :]
        m_out[...] = dot(r_inv, ui[...])
        ri_out[...] = r_inv * s_out[...]

    sq = jax.ShapeDtypeStruct((NB, NB), jnp.float32)
    return pl.pallas_call(
        kernel,
        out_shape=[sq, sq, sq, sq, sq, jax.ShapeDtypeStruct((1, NB), jnp.float32)],
        scratch_shapes=[
            pltpu.VMEM((3 * NB, NB), jnp.float32),
            pltpu.VMEM((NB, BK), jnp.float32),
            pltpu.VMEM((NB, NB), jnp.float32),
        ],
        compiler_params=pltpu.CompilerParams(vmem_limit_bytes=24 * 1024 * 1024),
        cost_estimate=pl.CostEstimate(flops=20_000_000_000, bytes_accessed=2_000_000, transcendentals=0),
        name="factor",
    )(gram, top)


def mm(left, right, ca=1, cb=0, precision=lax.Precision.HIGH):
    return lax.dot_general(
        left, right, (((ca,), (cb,)), ((), ())), precision=precision, preferred_element_type=jnp.float32
    )


XS, ZS, RS = 4, 8, 8
X_GROUPS = [[z * XS + x for x in range(XS)] for z in range(ZS)]
Z_GROUPS = [[z * XS + x for z in range(ZS)] for x in range(XS)]


def exchange(value, axis, groups=None):
    return lax.all_to_all(value, axis, 0, 0, tiled=True, axis_index_groups=groups)


def to_all(value, count, axis, groups=None):
    return exchange(jnp.broadcast_to(value[None], (count, *value.shape)), axis, groups)


def x_shift(value, k):
    pairs = [(z * XS + x, z * XS + (x + k) % XS) for z in range(ZS) for x in range(XS)]
    return lax.ppermute(value, "col", pairs)


def swap(value):
    cols = ZS * XS
    pairs = [
        (r * cols + z * XS + x, z * cols + r * XS + x)
        for r in range(RS)
        for z in range(ZS)
        for x in range(XS)
    ]
    return lax.ppermute(value, ("row", "col"), pairs)


def gather_x(value):
    shifted = {k: x_shift(value, k) for k in (2, 1, 3)}
    return [value, shifted[1], shifted[2], shifted[3]]


def split(value):
    high = value.astype(jnp.bfloat16)
    return high, (value - high.astype(jnp.float32)).astype(jnp.bfloat16)


def dot_split(left, right):
    def one(a, b):
        return lax.dot_general(a, b, (((1,), (1,)), ((), ())), preferred_element_type=jnp.float32)

    return one(left[0], right[0]) + (one(left[0], right[1]) + one(left[1], right[0]))


def update(x_index, matrix, v_parts, x_parts, v_cols, arrived, inner, t_factor, v_own, x_own):
    rows, cols = matrix.shape
    quarter = rows // XS
    share, piece = NB // RS, cols // RS

    def kernel(at, a_ref, *refs):
        v_refs, x_refs = refs[:XS], refs[XS : 2 * XS]
        vc_ref, got_ref, inner_ref, t_ref, vo_ref, xo_ref, out_ref, w_ref, ys, vs = refs[2 * XS :]
        step = pl.program_id(0)

        @pl.when(step == 0)
        def _():
            core = dot(t_ref[...], inner_ref[...], 0, 0)
            w_ref[...] = xo_ref[...] - 0.5 * dot(vo_ref[...], core)
            even = split(0.5 * (core + core.T))
            vs[0], vs[1] = split(vc_ref[...])
            change = dot_split((vs[0], vs[1]), even)
            for r in range(RS):
                at_rows = slice(r * piece, (r + 1) * piece)
                ys[0, at_rows], ys[1, at_rows] = split(got_ref[r, share:] - change[at_rows])

        for j in range(XS):

            @pl.when(step == j)
            def _(j=j):
                out = a_ref[...] - dot_split(split(v_refs[j][...]), (ys[0], ys[1]))
                out_ref[...] = out - dot_split(split(x_refs[j][...]), (vs[0], vs[1]))

    def whole(array):
        return pl.BlockSpec(array.shape, lambda j, at: (0,) * array.ndim)

    block = pl.BlockSpec((quarter, cols), lambda j, at: ((at[0] + XS - j) % XS, 0))
    others = [*v_parts, *x_parts, v_cols, arrived, inner, t_factor, v_own, x_own]
    return pl.pallas_call(
        kernel,
        grid_spec=pltpu.PrefetchScalarGridSpec(
            num_scalar_prefetch=1,
            grid=(XS,),
            in_specs=[block] + [whole(array) for array in others],
            out_specs=[block, whole(x_own)],
            scratch_shapes=[pltpu.VMEM((2, cols, NB), jnp.bfloat16)] * 2,
        ),
        out_shape=[
            jax.ShapeDtypeStruct((rows, cols), jnp.float32),
            jax.ShapeDtypeStruct(x_own.shape, jnp.float32),
        ],
        compiler_params=pltpu.CompilerParams(vmem_limit_bytes=32 * 1024 * 1024),
        cost_estimate=pl.CostEstimate(flops=6_000_000_000, bytes_accessed=16_000_000, transcendentals=0),
        name="update",
    )(x_index[None], matrix, *others)


def body(matrix):
    rows, cols = matrix.shape
    row_index = lax.axis_index("row")
    col_index = lax.axis_index("col")
    z_index, x_index = col_index // XS, col_index % XS
    piece = cols // RS
    quarter = rows // XS
    share = NB // RS

    turned = matrix[: 2 * NB, :].T
    col_ids = col_index * cols + jnp.arange(cols)
    strip_turned = jnp.where((col_ids >= NB)[:, None], turned[:, :NB], 0.0)
    pieces = jnp.concatenate(
        [strip_turned.reshape(RS, piece, NB), turned[:, NB:].reshape(RS, piece, NB)], axis=1
    )
    pieces = exchange(pieces, "row")[0]
    strip_piece = pieces[:piece]
    strip_cols = to_all(strip_piece, RS, "row").reshape(cols, NB)
    pieces = swap(pieces)
    strip_moved, next_piece = pieces[:piece], pieces[piece:]

    own_cols = lax.dynamic_slice_in_dim(strip_cols, row_index * share, share, 1)
    gram_share = mm(own_cols, strip_cols, 0, 0, HI)
    top_share = lax.dynamic_slice_in_dim(strip_cols, NB + row_index * share, share, 0)
    small = jnp.concatenate([gram_share, jnp.where(col_index == 0, top_share, 0.0)], axis=0)
    small = jnp.sum(to_all(small, XS, "col", X_GROUPS), axis=0)
    small = jnp.sum(to_all(small, ZS, "col", Z_GROUPS), axis=0)
    small = to_all(small, RS, "row")
    gram_sum = small[:, :share].reshape(NB, NB)
    top_block = small[:, share:].reshape(NB, NB)
    low, up, low_inv, to_v, to_x, sign = factor_all(gram_sum, top_block)

    def partial(k):
        start = (x_index + k) % XS * quarter
        return mm(lax.dynamic_slice_in_dim(matrix, start, quarter, 0), strip_cols)

    prod = x_shift(partial(2), 2) + x_shift(partial(1), 1) + x_shift(partial(3), 3) + partial(0)
    both = jnp.concatenate(
        [prod.reshape(ZS, piece, NB), jnp.broadcast_to(strip_moved[None], (ZS, piece, NB))], axis=1
    )
    both = exchange(both, "col", Z_GROUPS)
    prod = jnp.sum(both[:, :piece], axis=0)
    strip_some = both[:, piece:].reshape(quarter, NB)
    strip_parts = gather_x(strip_some)

    x_piece = mm(mm(prod, to_x, 1, 0, HI) + next_piece, low_inv, 1, 1, HI)
    x_moved = swap(x_piece)
    x_some = to_all(x_piece, ZS, "col", Z_GROUPS).reshape(quarter, NB)
    x_parts = gather_x(x_some)

    low_placed = jnp.concatenate([jnp.zeros((quarter - NB, NB), jnp.float32), low], axis=0)
    late = (jnp.arange(quarter) >= quarter - NB)[:, None]

    def reflectors(strip, holds_top):
        return jnp.where(late & holds_top, low_placed, mm(strip, to_v))

    v_parts = [
        reflectors(part, (row_index == 0) & (x_index == k)) for k, part in enumerate(strip_parts)
    ]
    v_cols = reflectors(strip_cols, col_index == 0)
    inner = mm(lax.dynamic_slice_in_dim(v_parts[0], z_index * share, share, 1), x_some, 0, 0)
    inner = jnp.sum(to_all(inner, XS, "col", X_GROUPS), axis=0)
    arrived = to_all(jnp.concatenate([inner, x_moved], axis=0), RS, "row")
    inner = jnp.sum(arrived[:, :share], axis=0)
    inner = to_all(inner, ZS, "col", Z_GROUPS).reshape(NB, NB)
    t_factor = mm(up * sign, low_inv, 1, 1, HI)

    out_rows = rows // (XS * ZS)
    out_start = col_index * out_rows
    mine = (x_index + XS - out_start // quarter) % XS

    def own(parts):
        cut = [lax.dynamic_slice_in_dim(part, out_start % quarter, out_rows, 0) for part in parts]
        return jnp.where(mine < 2, jnp.where(mine == 0, cut[0], cut[1]), jnp.where(mine == 2, cut[2], cut[3]))

    v_own = own(v_parts)
    updated, w_own = update(
        x_index, matrix, v_parts, x_parts, v_cols, arrived, inner, t_factor, v_own, own(x_parts)
    )
    return (updated, v_own[None], w_own[None])


def solution(mesh):
    return jax.shard_map(
        body,
        mesh=mesh,
        in_specs=(P("row", "col"),),
        out_specs=(P("row", "col"), P(None, ("row", "col"), None), P(None, ("row", "col"), None)),
        check_vma=False,
    )
```

profile of v0, /device:TPU:42, one launch (start us, length us, event | category | flops | bytes accessed | tf_op | source)
XLA Modules:
  0.0 229.3 jit_solution(16764168293745205337)
XLA Ops:
  0.6 1.3 slice.38
  2.5 19.4 %all_to_all.50 = f32[8,128,256]{2,1,0:T(8,128)S(1)} all-to-all(f32[8,128,256]{2,1,0:T(8,128)S(1)} %pad_maximum_fusion), channel_id=1, replica_groups=mesh['row'=8,'col'=32] {'row'}, dimensions={0} | all-to-all | bytes 2097152 | tf_op jit(solution)/shard_map/all_to_all | solution.py:173
  22.7 4.9 %all-to-all-start.1 = ((f32[8,64,256]{2,1,0:T(8,128)}), f32[8,64,256]{2,1,0:T(8,128)S(1)}, u32[]{:S(2)}, u32[]{:S(2)}) async-start(f32[8,64,256]{2,1,0:T(8,128)} %broadcast_in_dim.117), calls=%async_computation.1 | async-start | bytes 1048576 | tf_op jit(solution)/shard_map/all_to_all | solution.py:173
  27.6 8.9 %all-to-all-done.1 = f32[8,64,256]{2,1,0:T(8,128)S(1)} async-done(((f32[8,64,256]{2,1,0:T(8,128)}), f32[8,64,256]{2,1,0:T(8,128)S(1)}, u32[]{:S(2)}, u32[]{:S(2)}) %all-to-all-start.1) | async-done | bytes 524320 | tf_op jit(solution)/shard_map/all_to_all | solution.py:173
  37.9 4.8 %all-to-all-start.2 = ((f32[4,64,256]{2,1,0:T(8,128)}), f32[4,64,256]{2,1,0:T(8,128)S(1)}, u32[]{:S(2)}, u32[]{:S(2)}) async-start(f32[4,64,256]{2,1,0:T(8,128)} %broadcast_in_dim.119), calls=%async_computation.2 | async-start | bytes 524288 | tf_op jit(solution)/shard_map/all_to_all | solution.py:173
  42.8 1.8 fusion.2
  44.6 3.4 %all-to-all-done.2 = f32[4,64,256]{2,1,0:T(8,128)S(1)} async-done(((f32[4,64,256]{2,1,0:T(8,128)}), f32[4,64,256]{2,1,0:T(8,128)S(1)}, u32[]{:S(2)}, u32[]{:S(2)}) %all-to-all-start.2) | async-done | bytes 262176 | tf_op jit(solution)/shard_map/all_to_all | solution.py:173
  48.8 8.6 %all-to-all-start.3 = ((f32[8,64,256]{2,1,0:T(8,128)}), f32[8,64,256]{2,1,0:T(8,128)S(1)}, u32[]{:S(2)}, u32[]{:S(2)}) async-start(f32[8,64,256]{2,1,0:T(8,128)} %broadcast_in_dim.120), calls=%async_computation.3 | async-start | bytes 1048576 | tf_op jit(solution)/shard_map/all_to_all | solution.py:173
  57.4 1.8 fusion.4
  59.2 2.6 %fusion.6 = f32[512,256]{1,0:T(8,128)} fusion(f32[512,256]{1,0:T(8,128)S(1)} %bitcast.52, f32[2048,512]{1,0:T(8,128)} %a_ref.1, s32[]{:T(128)S(6)} %select_n.150), kind=kOutput, calls=%fused_computation.13 | convolution fusion | flops 402653184 | bytes 2097156 | tf_op jit(solution)/shard_map/dot_general | solution.py:162
  61.8 1.5 collective-permute-start
  63.3 1.5 collective-permute-start.1
  65.3 1.9 collective-permute-start.3
  67.3 5.1 %all-to-all-done.3 = f32[8,64,256]{2,1,0:T(8,128)S(1)} async-done(((f32[8,64,256]{2,1,0:T(8,128)}), f32[8,64,256]{2,1,0:T(8,128)S(1)}, u32[]{:S(2)}, u32[]{:S(2)}) %all-to-all-start.3) | async-done | bytes 524320 | tf_op jit(solution)/shard_map/all_to_all | solution.py:173
  73.3 5.1 %all-to-all-start.4 = ((f32[8,64,256]{2,1,0:T(8,128)}), f32[8,64,256]{2,1,0:T(8,128)S(1)}, u32[]{:S(2)}, u32[]{:S(2)}) async-start(f32[8,64,256]{2,1,0:T(8,128)} %broadcast_in_dim.121), calls=%async_computation.4 | async-start | bytes 1048576 | tf_op jit(solution)/shard_map/all_to_all | solution.py:173
  79.2 5.8 %collective-permute-done.1 = f32[512,256]{1,0:T(8,128)} collective-permute-done((f32[512,256]{1,0:T(8,128)S(1)}, f32[512,256]{1,0:T(8,128)}, u32[]{:S(2)}, u32[]{:S(2)}) %collective-permute-start.1) | collective-permute-done | bytes 524320 | tf_op jit(solution)/shard_map/ppermute | solution.py:182
  84.9 1.5 collective-permute-done.2
  86.4 2.3 add_add_fusion
  88.7 1.1 pad_maximum_fusion.1
  89.8 7.2 %all-to-all-start.5 = ((f32[8,128,256]{2,1,0:T(8,128)}), f32[8,128,256]{2,1,0:T(8,128)}, u32[]{:S(2)}, u32[]{:S(2)}) async-start(f32[8,128,256]{2,1,0:T(8,128)} %pad_maximum_fusion.1), calls=%async_computation.5 | async-start | bytes 2097152 | tf_op jit(solution)/shard_map/all_to_all | solution.py:173
  97.1 19.1 %factor.1 = (f32[256,256]{1,0:T(8,128)S(1)}, f32[256,256]{1,0:T(8,128)S(1)}, f32[256,256]{1,0:T(8,128)S(1)}, f32[256,256]{1,0:T(8,128)S(1)}, f32[256,256]{1,0:T(8,128)S(1)}, /*index=5*/f32[1,256]{1,0:T(1,128)S(1)}) custom-call(f32[256,256]{1,0:T(8,128)S(1)} %bitcast.45, f32[256,256]{1,0:T(8,128)S(1)} %bitcast.44), custom_call_target="tpu_custom_call" | custom-call | flops 20000000000 | bytes 2000000 | tf_op jit(solution)/shard_map/factor/pallas_call | solution.py:147
  116.2 8.4 %all-to-all-done.5 = f32[8,128,256]{2,1,0:T(8,128)} async-done(((f32[8,128,256]{2,1,0:T(8,128)}), f32[8,128,256]{2,1,0:T(8,128)}, u32[]{:S(2)}, u32[]{:S(2)}) %all-to-all-start.5) | async-done | bytes 1048608 | tf_op jit(solution)/shard_map/all_to_all | solution.py:173
  124.6 2.1 slice_reduce_fusion
  128.1 4.9 %all-to-all-start.6 = ((f32[8,64,256]{2,1,0:T(8,128)}), f32[8,64,256]{2,1,0:T(8,128)S(1)}, u32[]{:S(2)}, u32[]{:S(2)}) async-start(f32[8,64,256]{2,1,0:T(8,128)} %broadcast_in_dim.126), calls=%async_computation.6 | async-start | bytes 1048576 | tf_op jit(solution)/shard_map/all_to_all | solution.py:173
  133.1 3.6 %collective-permute-start.10 = (f32[64,256]{1,0:T(8,128)S(1)}, f32[64,256]{1,0:T(8,128)S(1)}, u32[]{:S(2)}, u32[]{:S(2)}) collective-permute-start(f32[64,256]{1,0:T(8,128)S(1)} %fusion.15), channel_id=1, source_target_pairs={{0,0},{1,1},{2,2},{3,3},{4,32},{5,33},{6,34},{7,35},{8,64},{9,65},... | collective-permute-start | bytes 196616 | tf_op jit(solution)/shard_map/ppermute | solution.py:193
  136.8 1.4 convolution_select_fusion.4.refs_0_
  138.3 14.8 %all-to-all-done.6 = f32[8,64,256]{2,1,0:T(8,128)S(1)} async-done(((f32[8,64,256]{2,1,0:T(8,128)}), f32[8,64,256]{2,1,0:T(8,128)S(1)}, u32[]{:S(2)}, u32[]{:S(2)}) %all-to-all-start.6) | async-done | bytes 524320 | tf_op jit(solution)/shard_map/all_to_all | solution.py:173
  154.2 4.2 %all-to-all-start.7 = ((f32[4,32,256]{2,1,0:T(8,128)}), f32[4,32,256]{2,1,0:T(8,128)S(1)}, u32[]{:S(2)}, u32[]{:S(2)}) async-start(f32[4,32,256]{2,1,0:T(8,128)} %broadcast_in_dim.128), calls=%async_computation.7 | async-start | bytes 262144 | tf_op jit(solution)/shard_map/all_to_all | solution.py:173
  158.4 1.2 convolution_select_fusion.refs_8_
  159.6 2.1 collective-permute-start.5
  161.7 9.3 %all-to-all-done.7 = f32[4,32,256]{2,1,0:T(8,128)S(1)} async-done(((f32[4,32,256]{2,1,0:T(8,128)}), f32[4,32,256]{2,1,0:T(8,128)S(1)}, u32[]{:S(2)}, u32[]{:S(2)}) %all-to-all-start.7) | async-done | bytes 131104 | tf_op jit(solution)/shard_map/all_to_all | solution.py:173
  171.1 0.9 broadcast_in_dim.129
  172.0 3.5 %all-to-all-start.8 = ((f32[8,96,256]{2,1,0:T(8,128)}), f32[8,96,256]{2,1,0:T(8,128)S(1)}, u32[]{:S(2)}, u32[]{:S(2)}) async-start(f32[8,96,256]{2,1,0:T(8,128)} %broadcast_in_dim.129), calls=%async_computation.8 | async-start | bytes 1572864 | tf_op jit(solution)/shard_map/all_to_all | solution.py:173
  175.6 1.1 fusion.8.refs_11_
  176.7 1.4 convolution_select_fusion.3.refs_1_
  178.2 3.9 %collective-permute-start.8 = (f32[512,256]{1,0:T(8,128)S(1)}, f32[512,256]{1,0:T(8,128)}, u32[]{:S(2)}, u32[]{:S(2)}) collective-permute-start(f32[512,256]{1,0:T(8,128)S(1)} %bitcast.40), channel_id=1, source_target_pairs={{0,2},{1,3},{2,0},{3,1},{4,6},{5,7},{6,4},{7,5},{8,10},{9,11},{10,... | collective-permute-start | bytes 1572872 | tf_op jit(solution)/shard_map/ppermute | solution.py:182
  182.1 2.5 %collective-permute-start.7 = (f32[512,256]{1,0:T(8,128)S(1)}, f32[512,256]{1,0:T(8,128)}, u32[]{:S(2)}, u32[]{:S(2)}) collective-permute-start(f32[512,256]{1,0:T(8,128)S(1)} %bitcast.41), channel_id=1, source_target_pairs={{0,1},{1,2},{2,3},{3,0},{4,5},{5,6},{6,7},{7,4},{8,9},{9,10},{10,1... | collective-permute-start | bytes 1572872 | tf_op jit(solution)/shard_map/ppermute | solution.py:182
  184.6 1.4 convolution_select_fusion.2.refs_2_
  186.0 1.1 all-to-all-done.8.refs_9_
  187.8 4.2 %all-to-all-start.9 = ((f32[8,32,256]{2,1,0:T(8,128)}), f32[8,32,256]{2,1,0:T(8,128)}, u32[]{:S(2)}, u32[]{:S(2)}) async-start(f32[8,32,256]{2,1,0:T(8,128)} %broadcast_in_dim.130), calls=%async_computation.9 | async-start | bytes 524288 | tf_op jit(solution)/shard_map/all_to_all | solution.py:173
  192.1 1.4 convolution_select_fusion.1.refs_3_
  194.4 8.2 %collective-permute-done.9.refs_7_ = f32[512,256]{1,0:T(8,128)} collective-permute-done((f32[512,256]{1,0:T(8,128)S(1)}, f32[512,256]{1,0:T(8,128)}, u32[]{:S(2)}, u32[]{:S(2)}) %collective-permute-start.9) | collective-permute-done | bytes 524320 | tf_op jit(solution)/shard_map/ppermute | solution.py:182
  202.6 12.4 %collective-permute-done.8.refs_6_ = f32[512,256]{1,0:T(8,128)} collective-permute-done((f32[512,256]{1,0:T(8,128)S(1)}, f32[512,256]{1,0:T(8,128)}, u32[]{:S(2)}, u32[]{:S(2)}) %collective-permute-start.8) | collective-permute-done | bytes 524320 | tf_op jit(solution)/shard_map/ppermute | solution.py:182
  216.0 2.2 copy-done
  218.2 1.0 copy-done.2
  219.2 1.0 copy-done.3
  220.2 0.9 copy-done.4
  221.2 8.1 %update.1 = (f32[2048,512]{1,0:T(8,128)}, f32[64,256]{1,0:T(8,128)}) custom-call(s32[1]{0:T(128)} %bitcast.at, f32[2048,512]{1,0:T(8,128)S(1)} %copy-done, f32[512,256]{1,0:T(8,128)S(1)} %convolution_select_fusion.4.refs_0_, f32[512,256]{1,0:T(8,128)S(1)} %convolution_select_fusion.3.refs_1_, f32[512,256]{1,0:T(8,128)S(1)} %convolution_select_fusion.2.refs_2_, ...), custom_call_target="tpu_custom_call" | custom-call | flops 6000000000 | bytes 16000000 | tf_op jit(solution)/shard_map/update/pallas_call | solution.py:246
  (55 shorter events, 11.3 us)
Async XLA Ops:
  22.7 13.8 %all-to-all-start.1 = ((f32[8,64,256]{2,1,0:T(8,128)}), f32[8,64,256]{2,1,0:T(8,128)S(1)}, u32[]{:S(2)}, u32[]{:S(2)}) async-start(f32[8,64,256]{2,1,0:T(8,128)} %broadcast_in_dim.117), calls=%async_computation.1 | async-start | bytes 1048576 | tf_op jit(solution)/shard_map/all_to_all | solution.py:173
  37.9 10.0 %all-to-all-start.2 = ((f32[4,64,256]{2,1,0:T(8,128)}), f32[4,64,256]{2,1,0:T(8,128)S(1)}, u32[]{:S(2)}, u32[]{:S(2)}) async-start(f32[4,64,256]{2,1,0:T(8,128)} %broadcast_in_dim.119), calls=%async_computation.2 | async-start | bytes 524288 | tf_op jit(solution)/shard_map/all_to_all | solution.py:173
  48.8 23.6 %all-to-all-start.3 = ((f32[8,64,256]{2,1,0:T(8,128)}), f32[8,64,256]{2,1,0:T(8,128)S(1)}, u32[]{:S(2)}, u32[]{:S(2)}) async-start(f32[8,64,256]{2,1,0:T(8,128)} %broadcast_in_dim.120), calls=%async_computation.3 | async-start | bytes 1048576 | tf_op jit(solution)/shard_map/all_to_all | solution.py:173
  61.8 17.3 %collective-permute-start = (f32[512,256]{1,0:T(8,128)}, f32[512,256]{1,0:T(8,128)}, u32[]{:S(2)}, u32[]{:S(2)}) collective-permute-start(f32[512,256]{1,0:T(8,128)} %fusion.6), channel_id=1, source_target_pairs={{0,2},{1,3},{2,0},{3,1},{4,6},{5,7},{6,4},{7,5},{8,10},{9,11},{10,... | collective-permute-start | bytes 1572872 | tf_op jit(solution)/shard_map/ppermute | solution.py:182
  63.3 21.6 %collective-permute-start.1 = (f32[512,256]{1,0:T(8,128)S(1)}, f32[512,256]{1,0:T(8,128)}, u32[]{:S(2)}, u32[]{:S(2)}) collective-permute-start(f32[512,256]{1,0:T(8,128)S(1)} %fusion.4), channel_id=1, source_target_pairs={{0,1},{1,2},{2,3},{3,0},{4,5},{5,6},{6,7},{7,4},{8,9},{9,10},{10,1... | collective-permute-start | bytes 1572872 | tf_op jit(solution)/shard_map/ppermute | solution.py:182
  64.8 21.6 %collective-permute-start.2 = (f32[512,256]{1,0:T(8,128)S(1)}, f32[512,256]{1,0:T(8,128)}, u32[]{:S(2)}, u32[]{:S(2)}) collective-permute-start(f32[512,256]{1,0:T(8,128)S(1)} %fusion.2), channel_id=1, source_target_pairs={{0,3},{1,0},{2,1},{3,2},{4,7},{5,4},{6,5},{7,6},{8,11},{9,8},{10,9... | collective-permute-start | bytes 1572872 | tf_op jit(solution)/shard_map/ppermute | solution.py:182
  65.3 13.8 %collective-permute-start.3 = (f32[128,256]{1,0:T(8,128)S(1)}, f32[128,256]{1,0:T(8,128)S(1)}, u32[]{:S(2)}, u32[]{:S(2)}) collective-permute-start(f32[128,256]{1,0:T(8,128)S(1)} %slice_bitcast_fusion), channel_id=1, source_target_pairs={{0,0},{1,1},{2,2},{3,3},{4,32},{5,33},{6,34},{7,35},{8,64},{9,65},... | collective-permute-start | bytes 393224 | tf_op jit(solution)/shard_map/ppermute | solution.py:193
  73.3 16.5 %all-to-all-start.4 = ((f32[8,64,256]{2,1,0:T(8,128)}), f32[8,64,256]{2,1,0:T(8,128)S(1)}, u32[]{:S(2)}, u32[]{:S(2)}) async-start(f32[8,64,256]{2,1,0:T(8,128)} %broadcast_in_dim.121), calls=%async_computation.4 | async-start | bytes 1048576 | tf_op jit(solution)/shard_map/all_to_all | solution.py:173
  89.8 34.8 %all-to-all-start.5 = ((f32[8,128,256]{2,1,0:T(8,128)}), f32[8,128,256]{2,1,0:T(8,128)}, u32[]{:S(2)}, u32[]{:S(2)}) async-start(f32[8,128,256]{2,1,0:T(8,128)} %pad_maximum_fusion.1), calls=%async_computation.5 | async-start | bytes 2097152 | tf_op jit(solution)/shard_map/all_to_all | solution.py:173
  128.1 24.9 %all-to-all-start.6 = ((f32[8,64,256]{2,1,0:T(8,128)}), f32[8,64,256]{2,1,0:T(8,128)S(1)}, u32[]{:S(2)}, u32[]{:S(2)}) async-start(f32[8,64,256]{2,1,0:T(8,128)} %broadcast_in_dim.126), calls=%async_computation.6 | async-start | bytes 1048576 | tf_op jit(solution)/shard_map/all_to_all | solution.py:173
  133.1 38.0 %collective-permute-start.10 = (f32[64,256]{1,0:T(8,128)S(1)}, f32[64,256]{1,0:T(8,128)S(1)}, u32[]{:S(2)}, u32[]{:S(2)}) collective-permute-start(f32[64,256]{1,0:T(8,128)S(1)} %fusion.15), channel_id=1, source_target_pairs={{0,0},{1,1},{2,2},{3,3},{4,32},{5,33},{6,34},{7,35},{8,64},{9,65},... | collective-permute-start | bytes 196616 | tf_op jit(solution)/shard_map/ppermute | solution.py:193
  136.7 40.0 %collective-permute-start.4 = (f32[512,256]{1,0:T(8,128)}, f32[512,256]{1,0:T(8,128)}, u32[]{:S(2)}, u32[]{:S(2)}) collective-permute-start(f32[512,256]{1,0:T(8,128)} %bitcast.10), channel_id=1, source_target_pairs={{0,1},{1,2},{2,3},{3,0},{4,5},{5,6},{6,7},{7,4},{8,9},{9,10},{10,1... | collective-permute-start | bytes 1572872 | tf_op jit(solution)/shard_map/ppermute | solution.py:182
  154.2 16.8 %all-to-all-start.7 = ((f32[4,32,256]{2,1,0:T(8,128)}), f32[4,32,256]{2,1,0:T(8,128)S(1)}, u32[]{:S(2)}, u32[]{:S(2)}) async-start(f32[4,32,256]{2,1,0:T(8,128)} %broadcast_in_dim.128), calls=%async_computation.7 | async-start | bytes 262144 | tf_op jit(solution)/shard_map/all_to_all | solution.py:173
  159.6 25.0 %collective-permute-start.5 = (f32[512,256]{1,0:T(8,128)}, f32[512,256]{1,0:T(8,128)}, u32[]{:S(2)}, u32[]{:S(2)}) collective-permute-start(f32[512,256]{1,0:T(8,128)} %bitcast.10), channel_id=1, source_target_pairs={{0,2},{1,3},{2,0},{3,1},{4,6},{5,7},{6,4},{7,5},{8,10},{9,11},{10,... | collective-permute-start | bytes 1572872 | tf_op jit(solution)/shard_map/ppermute | solution.py:182
  172.0 15.1 %all-to-all-start.8 = ((f32[8,96,256]{2,1,0:T(8,128)}), f32[8,96,256]{2,1,0:T(8,128)S(1)}, u32[]{:S(2)}, u32[]{:S(2)}) async-start(f32[8,96,256]{2,1,0:T(8,128)} %broadcast_in_dim.129), calls=%async_computation.8 | async-start | bytes 1572864 | tf_op jit(solution)/shard_map/all_to_all | solution.py:173
  176.7 15.4 %collective-permute-start.6 = (f32[512,256]{1,0:T(8,128)}, f32[512,256]{1,0:T(8,128)}, u32[]{:S(2)}, u32[]{:S(2)}) collective-permute-start(f32[512,256]{1,0:T(8,128)} %bitcast.10), channel_id=1, source_target_pairs={{0,3},{1,0},{2,1},{3,2},{4,7},{5,4},{6,5},{7,6},{8,11},{9,8},{10,9... | collective-permute-start | bytes 1572872 | tf_op jit(solution)/shard_map/ppermute | solution.py:182
  178.1 24.5 %collective-permute-start.9 = (f32[512,256]{1,0:T(8,128)S(1)}, f32[512,256]{1,0:T(8,128)}, u32[]{:S(2)}, u32[]{:S(2)}) collective-permute-start(f32[512,256]{1,0:T(8,128)S(1)} %bitcast.39), channel_id=1, source_target_pairs={{0,3},{1,0},{2,1},{3,2},{4,7},{5,4},{6,5},{7,6},{8,11},{9,8},{10,9... | collective-permute-start | bytes 1572872 | tf_op jit(solution)/shard_map/ppermute | solution.py:182
  178.2 36.8 %collective-permute-start.8 = (f32[512,256]{1,0:T(8,128)S(1)}, f32[512,256]{1,0:T(8,128)}, u32[]{:S(2)}, u32[]{:S(2)}) collective-permute-start(f32[512,256]{1,0:T(8,128)S(1)} %bitcast.40), channel_id=1, source_target_pairs={{0,2},{1,3},{2,0},{3,1},{4,6},{5,7},{6,4},{7,5},{8,10},{9,11},{10,... | collective-permute-start | bytes 1572872 | tf_op jit(solution)/shard_map/ppermute | solution.py:182
  182.1 32.9 %collective-permute-start.7 = (f32[512,256]{1,0:T(8,128)S(1)}, f32[512,256]{1,0:T(8,128)}, u32[]{:S(2)}, u32[]{:S(2)}) collective-permute-start(f32[512,256]{1,0:T(8,128)S(1)} %bitcast.41), channel_id=1, source_target_pairs={{0,1},{1,2},{2,3},{3,0},{4,5},{5,6},{6,7},{7,4},{8,9},{9,10},{10,1... | collective-permute-start | bytes 1572872 | tf_op jit(solution)/shard_map/ppermute | solution.py:182
  187.8 28.1 %all-to-all-start.9 = ((f32[8,32,256]{2,1,0:T(8,128)}), f32[8,32,256]{2,1,0:T(8,128)}, u32[]{:S(2)}, u32[]{:S(2)}) async-start(f32[8,32,256]{2,1,0:T(8,128)} %broadcast_in_dim.130), calls=%async_computation.9 | async-start | bytes 524288 | tf_op jit(solution)/shard_map/all_to_all | solution.py:173
  193.6 0.8 copy-start.1
  194.4 34.9 %copy-start.5 = (f32[64,256]{1,0:T(8,128)}, f32[64,256]{1,0:T(8,128)S(1)}, u32[]{:S(2)}) copy-start(f32[64,256]{1,0:T(8,128)S(1)} %select_select_fusion.1.refs_12_) | copy-start | bytes 196612
  216.0 2.2 copy-start
  218.1 1.0 copy-start.2
  219.2 1.0 copy-start.3
  220.2 0.9 copy-start.4
where the time goes:
time: 231 us; the launch traced here: 229 us
  waiting for transfers between devices  79.8 us (35%)
  starting transfers between devices  65.1 us (28%)
  Pallas kernels  27.2 us (12%)
  blocking collectives  19.4 us (8%)
  matrix products  18.3 us (8%)
  local copies, waits for them, and re-layouts  14.2 us (6%)
  other arithmetic  4.49 us (2%)
    all_to_all x9, waiting for transfers between devices, exchange(): lax.all_to_all(value, axis, 0, 0, tiled=True, axis_index_groups=groups)  51.1 us
    all_to_all x9, starting transfers between devices, exchange(): lax.all_to_all(value, axis, 0, 0, tiled=True, axis_index_groups=groups)  47.4 us
    ppermute x9, waiting for transfers between devices, x_shift(): return lax.ppermute(value, 'col', pairs)  27.9 us
    all_to_all x1, blocking collectives, exchange(): lax.all_to_all(value, axis, 0, 0, tiled=True, axis_index_groups=groups)  19.4 us
    pallas_call x1, Pallas kernels, factor_all(): pl.pallas_call(kernel, out_shape=[sq, sq, sq, sq, sq, jax.ShapeDtypeStruc...  19.1 us
    dot_general x14, matrix products, mm(): lax.dot_general(left, right, (((ca,), (cb,)), ((), ())), precision=precis...  18.3 us
    ppermute x9, starting transfers between devices, x_shift(): return lax.ppermute(value, 'col', pairs)  12.1 us
    pallas_call x1, Pallas kernels, update(): pl.pallas_call(kernel, grid_spec=pltpu.PrefetchScalarGridSpec(num_scalar_...  8.1 us
  transfers between devices with their start and end apart: 20, of which 12 were waited for; matrix products, arithmetic and copies ran while one was open for 10% of the time, Pallas kernels for 8%

commit v1 on v0

--- a/solution.py
+++ b/solution.py
@@ -256,7 +256,7 @@
             jax.ShapeDtypeStruct((rows, cols), jnp.float32),
             jax.ShapeDtypeStruct(x_own.shape, jnp.float32),
         ],
-        compiler_params=pltpu.CompilerParams(vmem_limit_bytes=32 * 1024 * 1024),
+        compiler_params=pltpu.CompilerParams(vmem_limit_bytes=56 * 1024 * 1024),
         cost_estimate=pl.CostEstimate(flops=6_000_000_000, bytes_accessed=16_000_000, transcendentals=0),
         name="update",
     )(x_index[None], matrix, *others)
@@ -279,7 +279,7 @@
     )
     pieces = exchange(pieces, "row")[0]
     strip_piece = pieces[:piece]
-    strip_cols = to_all(strip_piece, RS, "row").reshape(cols, NB)
+    strip_cols = lax.all_gather(strip_piece, "row", axis=0, tiled=True)
     pieces = swap(pieces)
     strip_moved, next_piece = pieces[:piece], pieces[piece:]
 

time: 231 us -> 221 us (0.957)
  the two profiles are of different devices: /device:TPU:42 before, /device:TPU:10 now
where the time goes in v1:
time: 221 us; the launch traced here: 219 us
  starting transfers between devices  76.6 us (35%)
  waiting for transfers between devices  69.4 us (31%)
  Pallas kernels  29.4 us (13%)
  matrix products  17.2 us (8%)
  blocking collectives  12.5 us (6%)
  local copies, waits for them, and re-layouts  7.46 us (3%)
  other arithmetic  5.61 us (3%)
    all_to_all x9, starting transfers between devices, exchange(): lax.all_to_all(value, axis, 0, 0, tiled=True, axis_index_groups=groups)  48.8 us
    all_to_all x9, waiting for transfers between devices, exchange(): lax.all_to_all(value, axis, 0, 0, tiled=True, axis_index_groups=groups)  45.5 us
    ppermute x9, waiting for transfers between devices, x_shift(): return lax.ppermute(value, 'col', pairs)  23.3 us
    pallas_call x1, Pallas kernels, factor_all(): pl.pallas_call(kernel, out_shape=[sq, sq, sq, sq, sq, jax.ShapeDtypeStruc...  19.1 us
    dot_general x14, matrix products, mm(): lax.dot_general(left, right, (((ca,), (cb,)), ((), ())), precision=precis...  17.2 us
    ppermute x9, starting transfers between devices, x_shift(): return lax.ppermute(value, 'col', pairs)  15.4 us
    all_gather x1, blocking collectives, body(): strip_cols = lax.all_gather(strip_piece, 'row', axis=0, tiled=True)  12.5 us
    ppermute x2, starting transfers between devices, swap(): return lax.ppermute(value, ('row', 'col'), pairs)  12.3 us
  transfers between devices with their start and end apart: 20, of which 12 were waited for; matrix products, arithmetic and copies ran while one was open for 11% of the time, Pallas kernels for 9%

profile of v1, /device:TPU:10, one launch (start us, length us, event | category | flops | bytes accessed | tf_op | source)
XLA Modules:
  0.0 219.1 jit_solution(1740399608551419803)
XLA Ops:
  0.6 1.3 slice_bitcast_fusion
  2.5 1.1 pad_maximum_fusion
  3.5 4.9 %all-to-all-start = ((f32[8,128,256]{2,1,0:T(8,128)}), f32[8,128,256]{2,1,0:T(8,128)S(1)}, u32[]{:S(2)}, u32[]{:S(2)}) async-start(f32[8,128,256]{2,1,0:T(8,128)} %pad_maximum_fusion), calls=%async_computation | async-start | bytes 2097152 | tf_op jit(solution)/shard_map/all_to_all | solution.py:173
  8.5 14.5 %all-to-all-done = f32[8,128,256]{2,1,0:T(8,128)S(1)} async-done(((f32[8,128,256]{2,1,0:T(8,128)}), f32[8,128,256]{2,1,0:T(8,128)S(1)}, u32[]{:S(2)}, u32[]{:S(2)}) %all-to-all-start) | async-done | bytes 1048608 | tf_op jit(solution)/shard_map/all_to_all | solution.py:173
  23.0 12.5 %all-gather = f32[1,512,256]{2,1,0:T(8,128)S(1)} all-gather(f32[1,64,256]{2,1,0:T(8,128)S(1)} %slice.55), channel_id=2, replica_groups=mesh['row'=8,'col'=32] {'row'}, dimensions={1}, use_global_device_ids=true | all-gather | bytes 589824 | tf_op jit(solution)/shard_map/all_gather | solution.py:282
  36.9 4.8 %all-to-all-start.1 = ((f32[4,64,256]{2,1,0:T(8,128)}), f32[4,64,256]{2,1,0:T(8,128)S(1)}, u32[]{:S(2)}, u32[]{:S(2)}) async-start(f32[4,64,256]{2,1,0:T(8,128)} %broadcast_in_dim.109), calls=%async_computation.1 | async-start | bytes 524288 | tf_op jit(solution)/shard_map/all_to_all | solution.py:173
  41.7 1.8 fusion.6
  43.5 4.0 %all-to-all-done.1 = f32[4,64,256]{2,1,0:T(8,128)S(1)} async-done(((f32[4,64,256]{2,1,0:T(8,128)}), f32[4,64,256]{2,1,0:T(8,128)S(1)}, u32[]{:S(2)}, u32[]{:S(2)}) %all-to-all-start.1) | async-done | bytes 262176 | tf_op jit(solution)/shard_map/all_to_all | solution.py:173
  47.6 0.8 broadcast_in_dim.110
  48.4 8.4 %all-to-all-start.2 = ((f32[8,64,256]{2,1,0:T(8,128)}), f32[8,64,256]{2,1,0:T(8,128)S(1)}, u32[]{:S(2)}, u32[]{:S(2)}) async-start(f32[8,64,256]{2,1,0:T(8,128)} %broadcast_in_dim.110), calls=%async_computation.2 | async-start | bytes 1048576 | tf_op jit(solution)/shard_map/all_to_all | solution.py:173
  56.8 1.8 fusion.4
  58.6 2.6 %fusion.2 = f32[512,256]{1,0:T(8,128)} fusion(f32[2048,512]{1,0:T(8,128)} %a_ref.1, s32[]{:T(128)S(6)} %select_n.154, f32[1,512,256]{2,1,0:T(8,128)S(1)} %all-gather), kind=kOutput, calls=%fused_computation.9 | convolution fusion | flops 402653184 | bytes 2097156 | tf_op jit(solution)/shard_map/dot_general | solution.py:162
  61.2 1.5 collective-permute-start.2
  63.2 2.7 %collective-permute-start = (f32[512,256]{1,0:T(8,128)S(1)}, f32[512,256]{1,0:T(8,128)}, u32[]{:S(2)}, u32[]{:S(2)}) collective-permute-start(f32[512,256]{1,0:T(8,128)S(1)} %fusion.6), channel_id=1, source_target_pairs={{0,2},{1,3},{2,0},{3,1},{4,6},{5,7},{6,4},{7,5},{8,10},{9,11},{10,... | collective-permute-start | bytes 1572872 | tf_op jit(solution)/shard_map/ppermute | solution.py:182
  65.9 6.3 %collective-permute-start.3 = (f32[128,256]{1,0:T(8,128)S(1)}, f32[128,256]{1,0:T(8,128)S(1)}, u32[]{:S(2)}, u32[]{:S(2)}) collective-permute-start(f32[128,256]{1,0:T(8,128)S(1)} %slice_bitcast_fusion.1), channel_id=1, source_target_pairs={{0,0},{1,1},{2,2},{3,3},{4,32},{5,33},{6,34},{7,35},{8,64},{9,65},... | collective-permute-start | bytes 393224 | tf_op jit(solution)/shard_map/ppermute | solution.py:193
  72.2 1.1 all-to-all-done.2
  73.4 0.8 broadcast_in_dim.111
  74.2 6.7 %all-to-all-start.3 = ((f32[8,64,256]{2,1,0:T(8,128)}), f32[8,64,256]{2,1,0:T(8,128)S(1)}, u32[]{:S(2)}, u32[]{:S(2)}) async-start(f32[8,64,256]{2,1,0:T(8,128)} %broadcast_in_dim.111), calls=%async_computation.3 | async-start | bytes 1048576 | tf_op jit(solution)/shard_map/all_to_all | solution.py:173
  81.6 3.7 %collective-permute-done.2 = f32[512,256]{1,0:T(8,128)} collective-permute-done((f32[512,256]{1,0:T(8,128)}, f32[512,256]{1,0:T(8,128)}, u32[]{:S(2)}, u32[]{:S(2)}) %collective-permute-start.2) | collective-permute-done | bytes 524320 | tf_op jit(solution)/shard_map/ppermute | solution.py:182
  85.2 2.3 %add_add_fusion = f32[512,256]{1,0:T(8,128)S(1)} fusion(f32[512,256]{1,0:T(8,128)} %collective-permute-done.2, f32[512,256]{1,0:T(8,128)} %collective-permute-done, f32[512,256]{1,0:T(8,128)} %collective-permute-done.1, f32[1,512,256]{2,1,0:T(8,128)S(1)} %all-gather, f32[2048,512]{1,0:T(8,128)} %a_ref.1, s32[]{:T(128)S(6)} %select_n.156), kind=kOutput, calls=%fused_computation.25 | convolution fusion | flops 403046400 | bytes 3670020 | tf_op jit(solution)/shard_map/dot_general | solution.py:162
  87.6 1.1 pad_maximum_fusion.1
  88.6 1.2 all-to-all-done.3
  89.9 5.7 %all-to-all-start.4 = ((f32[8,128,256]{2,1,0:T(8,128)}), f32[8,128,256]{2,1,0:T(8,128)S(1)}, u32[]{:S(2)}, u32[]{:S(2)}) async-start(f32[8,128,256]{2,1,0:T(8,128)} %pad_maximum_fusion.1), calls=%async_computation.4 | async-start | bytes 2097152 | tf_op jit(solution)/shard_map/all_to_all | solution.py:173
  95.6 19.1 %factor.1 = (f32[256,256]{1,0:T(8,128)S(1)}, f32[256,256]{1,0:T(8,128)S(1)}, f32[256,256]{1,0:T(8,128)S(1)}, f32[256,256]{1,0:T(8,128)S(1)}, f32[256,256]{1,0:T(8,128)S(1)}, /*index=5*/f32[1,256]{1,0:T(1,128)S(1)}) custom-call(f32[256,256]{1,0:T(8,128)S(1)} %bitcast.51, f32[256,256]{1,0:T(8,128)S(1)} %bitcast.50), custom_call_target="tpu_custom_call" | custom-call | flops 20000000000 | bytes 2000000 | tf_op jit(solution)/shard_map/factor/pallas_call | solution.py:147
  114.7 7.5 %all-to-all-done.4 = f32[8,128,256]{2,1,0:T(8,128)S(1)} async-done(((f32[8,128,256]{2,1,0:T(8,128)}), f32[8,128,256]{2,1,0:T(8,128)S(1)}, u32[]{:S(2)}, u32[]{:S(2)}) %all-to-all-start.4) | async-done | bytes 1048608 | tf_op jit(solution)/shard_map/all_to_all | solution.py:173
  123.7 3.5 %all-to-all-start.5 = ((f32[8,64,256]{2,1,0:T(8,128)}), f32[8,64,256]{2,1,0:T(8,128)S(1)}, u32[]{:S(2)}, u32[]{:S(2)}) async-start(f32[8,64,256]{2,1,0:T(8,128)} %broadcast_in_dim.116), calls=%async_computation.5 | async-start | bytes 1048576 | tf_op jit(solution)/shard_map/all_to_all | solution.py:173
  127.4 6.0 %collective-permute-start.10 = (f32[64,256]{1,0:T(8,128)S(1)}, f32[64,256]{1,0:T(8,128)S(1)}, u32[]{:S(2)}, u32[]{:S(2)}) collective-permute-start(f32[64,256]{1,0:T(8,128)S(1)} %fusion.22), channel_id=1, source_target_pairs={{0,0},{1,1},{2,2},{3,3},{4,32},{5,33},{6,34},{7,35},{8,64},{9,65},... | collective-permute-start | bytes 196616 | tf_op jit(solution)/shard_map/ppermute | solution.py:193
  133.4 2.2 collective-permute-start.4
  135.9 6.1 %all-to-all-done.5 = f32[8,64,256]{2,1,0:T(8,128)S(1)} async-done(((f32[8,64,256]{2,1,0:T(8,128)}), f32[8,64,256]{2,1,0:T(8,128)S(1)}, u32[]{:S(2)}, u32[]{:S(2)}) %all-to-all-start.5) | async-done | bytes 524320 | tf_op jit(solution)/shard_map/all_to_all | solution.py:173
  143.2 4.9 %all-to-all-start.6 = ((f32[4,32,256]{2,1,0:T(8,128)}), f32[4,32,256]{2,1,0:T(8,128)S(1)}, u32[]{:S(2)}, u32[]{:S(2)}) async-start(f32[4,32,256]{2,1,0:T(8,128)} %broadcast_in_dim.118), calls=%async_computation.6 | async-start | bytes 262144 | tf_op jit(solution)/shard_map/all_to_all | solution.py:173
  148.2 1.2 convolution_select_fusion.refs_8_
  149.3 2.1 collective-permute-start.5
  151.4 9.9 %all-to-all-done.6 = f32[4,32,256]{2,1,0:T(8,128)S(1)} async-done(((f32[4,32,256]{2,1,0:T(8,128)}), f32[4,32,256]{2,1,0:T(8,128)S(1)}, u32[]{:S(2)}, u32[]{:S(2)}) %all-to-all-start.6) | async-done | bytes 131104 | tf_op jit(solution)/shard_map/all_to_all | solution.py:173
  161.3 0.9 broadcast_in_dim.119
  162.3 5.6 %all-to-all-start.7 = ((f32[8,96,256]{2,1,0:T(8,128)}), f32[8,96,256]{2,1,0:T(8,128)S(1)}, u32[]{:S(2)}, u32[]{:S(2)}) async-start(f32[8,96,256]{2,1,0:T(8,128)} %broadcast_in_dim.119), calls=%async_computation.7 | async-start | bytes 1572864 | tf_op jit(solution)/shard_map/all_to_all | solution.py:173
  167.8 1.1 fusion.17.refs_11_
  168.9 1.4 convolution_select_fusion.3.refs_1_
  170.5 3.9 %collective-permute-start.8 = (f32[512,256]{1,0:T(8,128)S(1)}, f32[512,256]{1,0:T(8,128)}, u32[]{:S(2)}, u32[]{:S(2)}) collective-permute-start(f32[512,256]{1,0:T(8,128)S(1)} %bitcast.55), channel_id=1, source_target_pairs={{0,2},{1,3},{2,0},{3,1},{4,6},{5,7},{6,4},{7,5},{8,10},{9,11},{10,... | collective-permute-start | bytes 1572872 | tf_op jit(solution)/shard_map/ppermute | solution.py:182
  174.4 2.5 %collective-permute-start.7 = (f32[512,256]{1,0:T(8,128)S(1)}, f32[512,256]{1,0:T(8,128)}, u32[]{:S(2)}, u32[]{:S(2)}) collective-permute-start(f32[512,256]{1,0:T(8,128)S(1)} %bitcast.56), channel_id=1, source_target_pairs={{0,1},{1,2},{2,3},{3,0},{4,5},{5,6},{6,7},{7,4},{8,9},{9,10},{10,1... | collective-permute-start | bytes 1572872 | tf_op jit(solution)/shard_map/ppermute | solution.py:182
  176.9 1.4 convolution_select_fusion.2.refs_2_
  178.3 1.2 all-to-all-done.7.refs_9_
  180.4 4.3 %all-to-all-start.8 = ((f32[8,32,256]{2,1,0:T(8,128)}), f32[8,32,256]{2,1,0:T(8,128)}, u32[]{:S(2)}, u32[]{:S(2)}) async-start(f32[8,32,256]{2,1,0:T(8,128)} %broadcast_in_dim.120), calls=%async_computation.8 | async-start | bytes 524288 | tf_op jit(solution)/shard_map/all_to_all | solution.py:173
  184.7 1.4 convolution_select_fusion.1.refs_3_
  186.1 1.6 select_select_fusion.1.refs_12_
  187.7 7.2 %collective-permute-done.9.refs_7_ = f32[512,256]{1,0:T(8,128)} collective-permute-done((f32[512,256]{1,0:T(8,128)S(1)}, f32[512,256]{1,0:T(8,128)}, u32[]{:S(2)}, u32[]{:S(2)}) %collective-permute-start.9) | collective-permute-done | bytes 524320 | tf_op jit(solution)/shard_map/ppermute | solution.py:182
  194.9 12.4 %collective-permute-done.8.refs_6_ = f32[512,256]{1,0:T(8,128)} collective-permute-done((f32[512,256]{1,0:T(8,128)S(1)}, f32[512,256]{1,0:T(8,128)}, u32[]{:S(2)}, u32[]{:S(2)}) %collective-permute-start.8) | collective-permute-done | bytes 524320 | tf_op jit(solution)/shard_map/ppermute | solution.py:182
  207.3 1.5 select_select_fusion.refs_13_
  208.9 10.3 %update.1 = (f32[2048,512]{1,0:T(8,128)}, f32[64,256]{1,0:T(8,128)}) custom-call(s32[1]{0:T(128)} %bitcast.at, f32[2048,512]{1,0:T(8,128)} %a_ref.1, f32[512,256]{1,0:T(8,128)} %copy-done.2, f32[512,256]{1,0:T(8,128)} %copy-done.3, f32[512,256]{1,0:T(8,128)} %copy-done.4, f32[512,256]{1,0:T(8,128)} %copy-done.5, f32[512,256]{1,0:T(8,128)} %bitcast.58, ...), custom_call_target="tpu_custom_call" | custom-call | flops 6000000000 | bytes 16000000 | tf_op jit(solution)/shard_map/update/pallas_call | solution.py:246
  (55 shorter events, 7.3 us)
Async XLA Ops:
  3.5 19.4 %all-to-all-start = ((f32[8,128,256]{2,1,0:T(8,128)}), f32[8,128,256]{2,1,0:T(8,128)S(1)}, u32[]{:S(2)}, u32[]{:S(2)}) async-start(f32[8,128,256]{2,1,0:T(8,128)} %pad_maximum_fusion), calls=%async_computation | async-start | bytes 2097152 | tf_op jit(solution)/shard_map/all_to_all | solution.py:173
  36.9 10.7 %all-to-all-start.1 = ((f32[4,64,256]{2,1,0:T(8,128)}), f32[4,64,256]{2,1,0:T(8,128)S(1)}, u32[]{:S(2)}, u32[]{:S(2)}) async-start(f32[4,64,256]{2,1,0:T(8,128)} %broadcast_in_dim.109), calls=%async_computation.1 | async-start | bytes 524288 | tf_op jit(solution)/shard_map/all_to_all | solution.py:173
  48.4 25.0 %all-to-all-start.2 = ((f32[8,64,256]{2,1,0:T(8,128)}), f32[8,64,256]{2,1,0:T(8,128)S(1)}, u32[]{:S(2)}, u32[]{:S(2)}) async-start(f32[8,64,256]{2,1,0:T(8,128)} %broadcast_in_dim.110), calls=%async_computation.2 | async-start | bytes 1048576 | tf_op jit(solution)/shard_map/all_to_all | solution.py:173
  61.2 24.0 %collective-permute-start.2 = (f32[512,256]{1,0:T(8,128)}, f32[512,256]{1,0:T(8,128)}, u32[]{:S(2)}, u32[]{:S(2)}) collective-permute-start(f32[512,256]{1,0:T(8,128)} %fusion.2), channel_id=1, source_target_pairs={{0,3},{1,0},{2,1},{3,2},{4,7},{5,4},{6,5},{7,6},{8,11},{9,8},{10,9... | collective-permute-start | bytes 1572872 | tf_op jit(solution)/shard_map/ppermute | solution.py:182
  62.6 22.6 %collective-permute-start.1 = (f32[512,256]{1,0:T(8,128)S(1)}, f32[512,256]{1,0:T(8,128)}, u32[]{:S(2)}, u32[]{:S(2)}) collective-permute-start(f32[512,256]{1,0:T(8,128)S(1)} %fusion.4), channel_id=1, source_target_pairs={{0,1},{1,2},{2,3},{3,0},{4,5},{5,6},{6,7},{7,4},{8,9},{9,10},{10,1... | collective-permute-start | bytes 1572872 | tf_op jit(solution)/shard_map/ppermute | solution.py:182
  63.2 22.0 %collective-permute-start = (f32[512,256]{1,0:T(8,128)S(1)}, f32[512,256]{1,0:T(8,128)}, u32[]{:S(2)}, u32[]{:S(2)}) collective-permute-start(f32[512,256]{1,0:T(8,128)S(1)} %fusion.6), channel_id=1, source_target_pairs={{0,2},{1,3},{2,0},{3,1},{4,6},{5,7},{6,4},{7,5},{8,10},{9,11},{10,... | collective-permute-start | bytes 1572872 | tf_op jit(solution)/shard_map/ppermute | solution.py:182
  65.9 15.7 %collective-permute-start.3 = (f32[128,256]{1,0:T(8,128)S(1)}, f32[128,256]{1,0:T(8,128)S(1)}, u32[]{:S(2)}, u32[]{:S(2)}) collective-permute-start(f32[128,256]{1,0:T(8,128)S(1)} %slice_bitcast_fusion.1), channel_id=1, source_target_pairs={{0,0},{1,1},{2,2},{3,3},{4,32},{5,33},{6,34},{7,35},{8,64},{9,65},... | collective-permute-start | bytes 393224 | tf_op jit(solution)/shard_map/ppermute | solution.py:193
  74.2 15.6 %all-to-all-start.3 = ((f32[8,64,256]{2,1,0:T(8,128)}), f32[8,64,256]{2,1,0:T(8,128)S(1)}, u32[]{:S(2)}, u32[]{:S(2)}) async-start(f32[8,64,256]{2,1,0:T(8,128)} %broadcast_in_dim.111), calls=%async_computation.3 | async-start | bytes 1048576 | tf_op jit(solution)/shard_map/all_to_all | solution.py:173
  89.9 32.3 %all-to-all-start.4 = ((f32[8,128,256]{2,1,0:T(8,128)}), f32[8,128,256]{2,1,0:T(8,128)S(1)}, u32[]{:S(2)}, u32[]{:S(2)}) async-start(f32[8,128,256]{2,1,0:T(8,128)} %pad_maximum_fusion.1), calls=%async_computation.4 | async-start | bytes 2097152 | tf_op jit(solution)/shard_map/all_to_all | solution.py:173
  123.7 18.3 %all-to-all-start.5 = ((f32[8,64,256]{2,1,0:T(8,128)}), f32[8,64,256]{2,1,0:T(8,128)S(1)}, u32[]{:S(2)}, u32[]{:S(2)}) async-start(f32[8,64,256]{2,1,0:T(8,128)} %broadcast_in_dim.116), calls=%async_computation.5 | async-start | bytes 1048576 | tf_op jit(solution)/shard_map/all_to_all | solution.py:173
  127.4 33.9 %collective-permute-start.10 = (f32[64,256]{1,0:T(8,128)S(1)}, f32[64,256]{1,0:T(8,128)S(1)}, u32[]{:S(2)}, u32[]{:S(2)}) collective-permute-start(f32[64,256]{1,0:T(8,128)S(1)} %fusion.22), channel_id=1, source_target_pairs={{0,0},{1,1},{2,2},{3,3},{4,32},{5,33},{6,34},{7,35},{8,64},{9,65},... | collective-permute-start | bytes 196616 | tf_op jit(solution)/shard_map/ppermute | solution.py:193
  133.4 35.6 %collective-permute-start.4 = (f32[512,256]{1,0:T(8,128)S(1)}, f32[512,256]{1,0:T(8,128)}, u32[]{:S(2)}, u32[]{:S(2)}) collective-permute-start(f32[512,256]{1,0:T(8,128)S(1)} %bitcast.59), channel_id=1, source_target_pairs={{0,1},{1,2},{2,3},{3,0},{4,5},{5,6},{6,7},{7,4},{8,9},{9,10},{10,1... | collective-permute-start | bytes 1572872 | tf_op jit(solution)/shard_map/ppermute | solution.py:182
  135.9 26.3 %copy-start.2 = (f32[512,256]{1,0:T(8,128)}, f32[512,256]{1,0:T(8,128)S(1)}, u32[]{:S(2)}) copy-start(f32[512,256]{1,0:T(8,128)S(1)} %convolution_select_fusion.4.refs_0_) | copy-start | bytes 1572868
  142.1 65.2 %copy-start = (f32[8,64,256]{2,1,0:T(8,128)}, f32[8,64,256]{2,1,0:T(8,128)S(1)}, u32[]{:S(2)}) copy-start(f32[8,64,256]{2,1,0:T(8,128)S(1)} %all-to-all-done.5) | copy-start | bytes 1572868
  143.2 18.0 %all-to-all-start.6 = ((f32[4,32,256]{2,1,0:T(8,128)}), f32[4,32,256]{2,1,0:T(8,128)S(1)}, u32[]{:S(2)}, u32[]{:S(2)}) async-start(f32[4,32,256]{2,1,0:T(8,128)} %broadcast_in_dim.118), calls=%async_computation.6 | async-start | bytes 262144 | tf_op jit(solution)/shard_map/all_to_all | solution.py:173
  149.3 27.6 %collective-permute-start.5 = (f32[512,256]{1,0:T(8,128)S(1)}, f32[512,256]{1,0:T(8,128)}, u32[]{:S(2)}, u32[]{:S(2)}) collective-permute-start(f32[512,256]{1,0:T(8,128)S(1)} %bitcast.61), channel_id=1, source_target_pairs={{0,2},{1,3},{2,0},{3,1},{4,6},{5,7},{6,4},{7,5},{8,10},{9,11},{10,... | collective-permute-start | bytes 1572872 | tf_op jit(solution)/shard_map/ppermute | solution.py:182
  162.3 17.3 %all-to-all-start.7 = ((f32[8,96,256]{2,1,0:T(8,128)}), f32[8,96,256]{2,1,0:T(8,128)S(1)}, u32[]{:S(2)}, u32[]{:S(2)}) async-start(f32[8,96,256]{2,1,0:T(8,128)} %broadcast_in_dim.119), calls=%async_computation.7 | async-start | bytes 1572864 | tf_op jit(solution)/shard_map/all_to_all | solution.py:173
  168.9 15.7 %collective-permute-start.6 = (f32[512,256]{1,0:T(8,128)S(1)}, f32[512,256]{1,0:T(8,128)}, u32[]{:S(2)}, u32[]{:S(2)}) collective-permute-start(f32[512,256]{1,0:T(8,128)S(1)} %bitcast.62), channel_id=1, source_target_pairs={{0,3},{1,0},{2,1},{3,2},{4,7},{5,4},{6,5},{7,6},{8,11},{9,8},{10,9... | collective-permute-start | bytes 1572872 | tf_op jit(solution)/shard_map/ppermute | solution.py:182
  170.4 38.4 %copy-start.3 = (f32[512,256]{1,0:T(8,128)}, f32[512,256]{1,0:T(8,128)S(1)}, u32[]{:S(2)}) copy-start(f32[512,256]{1,0:T(8,128)S(1)} %convolution_select_fusion.3.refs_1_) | copy-start | bytes 1572868
  170.4 24.5 %collective-permute-start.9 = (f32[512,256]{1,0:T(8,128)S(1)}, f32[512,256]{1,0:T(8,128)}, u32[]{:S(2)}, u32[]{:S(2)}) collective-permute-start(f32[512,256]{1,0:T(8,128)S(1)} %bitcast.54), channel_id=1, source_target_pairs={{0,3},{1,0},{2,1},{3,2},{4,7},{5,4},{6,5},{7,6},{8,11},{9,8},{10,9... | collective-permute-start | bytes 1572872 | tf_op jit(solution)/shard_map/ppermute | solution.py:182
  170.5 36.8 %collective-permute-start.8 = (f32[512,256]{1,0:T(8,128)S(1)}, f32[512,256]{1,0:T(8,128)}, u32[]{:S(2)}, u32[]{:S(2)}) collective-permute-start(f32[512,256]{1,0:T(8,128)S(1)} %bitcast.55), channel_id=1, source_target_pairs={{0,2},{1,3},{2,0},{3,1},{4,6},{5,7},{6,4},{7,5},{8,10},{9,11},{10,... | collective-permute-start | bytes 1572872 | tf_op jit(solution)/shard_map/ppermute | solution.py:182
  174.4 32.9 %collective-permute-start.7 = (f32[512,256]{1,0:T(8,128)S(1)}, f32[512,256]{1,0:T(8,128)}, u32[]{:S(2)}, u32[]{:S(2)}) collective-permute-start(f32[512,256]{1,0:T(8,128)S(1)} %bitcast.56), channel_id=1, source_target_pairs={{0,1},{1,2},{2,3},{3,0},{4,5},{5,6},{6,7},{7,4},{8,9},{9,10},{10,1... | collective-permute-start | bytes 1572872 | tf_op jit(solution)/shard_map/ppermute | solution.py:182
  178.3 30.5 %copy-start.4 = (f32[512,256]{1,0:T(8,128)}, f32[512,256]{1,0:T(8,128)S(1)}, u32[]{:S(2)}) copy-start(f32[512,256]{1,0:T(8,128)S(1)} %convolution_select_fusion.2.refs_2_) | copy-start | bytes 1572868
  179.6 29.3 %copy-start.1 = (f32[8,96,256]{2,1,0:T(8,128)}, f32[8,96,256]{2,1,0:T(8,128)S(1)}, u32[]{:S(2)}) copy-start(f32[8,96,256]{2,1,0:T(8,128)S(1)} %all-to-all-done.7.refs_9_) | copy-start | bytes 2359300
  180.4 28.5 %all-to-all-start.8 = ((f32[8,32,256]{2,1,0:T(8,128)}), f32[8,32,256]{2,1,0:T(8,128)}, u32[]{:S(2)}, u32[]{:S(2)}) async-start(f32[8,32,256]{2,1,0:T(8,128)} %broadcast_in_dim.120), calls=%async_computation.8 | async-start | bytes 524288 | tf_op jit(solution)/shard_map/all_to_all | solution.py:173
  186.1 22.7 %copy-start.5 = (f32[512,256]{1,0:T(8,128)}, f32[512,256]{1,0:T(8,128)S(1)}, u32[]{:S(2)}) copy-start(f32[512,256]{1,0:T(8,128)S(1)} %convolution_select_fusion.1.refs_3_) | copy-start | bytes 1572868

commit v2 on v1

--- a/solution.py
+++ b/solution.py
@@ -210,20 +210,20 @@
     return one(left[0], right[0]) + (one(left[0], right[1]) + one(left[1], right[0]))
 
 
-def update(x_index, matrix, v_parts, x_parts, v_cols, arrived, inner, t_factor, v_own, x_own):
+def update(places, out_rows, matrix, v_parts, x_parts, v_cols, arrived, inner, t_factor):
     rows, cols = matrix.shape
     quarter = rows // XS
     share, piece = NB // RS, cols // RS
 
     def kernel(at, a_ref, *refs):
         v_refs, x_refs = refs[:XS], refs[XS : 2 * XS]
-        vc_ref, got_ref, inner_ref, t_ref, vo_ref, xo_ref, out_ref, w_ref, ys, vs = refs[2 * XS :]
+        vc_ref, got_ref, inner_ref, t_ref, out_ref, v_ref, w_ref, ys, vs, core_ref = refs[2 * XS :]
         step = pl.program_id(0)
 
         @pl.when(step == 0)
         def _():
             core = dot(t_ref[...], inner_ref[...], 0, 0)
-            w_ref[...] = xo_ref[...] - 0.5 * dot(vo_ref[...], core)
+            core_ref[...] = core
             even = split(0.5 * (core + core.T))
             vs[0], vs[1] = split(vc_ref[...])
             change = dot_split((vs[0], vs[1]), even)
@@ -238,28 +238,37 @@
                 out = a_ref[...] - dot_split(split(v_refs[j][...]), (ys[0], ys[1]))
                 out_ref[...] = out - dot_split(split(x_refs[j][...]), (vs[0], vs[1]))
 
+            @pl.when((step == j) & (at[1] == j))
+            def _(j=j):
+                mine = pl.ds(pl.multiple_of(at[2], out_rows), out_rows)
+                v_ref[...] = v_refs[j][mine]
+                w_ref[...] = x_refs[j][mine] - 0.5 * dot(v_refs[j][mine], core_ref[...])
+
     def whole(array):
         return pl.BlockSpec(array.shape, lambda j, at: (0,) * array.ndim)
 
     block = pl.BlockSpec((quarter, cols), lambda j, at: ((at[0] + XS - j) % XS, 0))
-    others = [*v_parts, *x_parts, v_cols, arrived, inner, t_factor, v_own, x_own]
+    others = [*v_parts, *x_parts, v_cols, arrived, inner, t_factor]
+    own = jax.ShapeDtypeStruct((out_rows, NB), jnp.float32)
     return pl.pallas_call(
         kernel,
         grid_spec=pltpu.PrefetchScalarGridSpec(
             num_scalar_prefetch=1,
             grid=(XS,),
             in_specs=[block] + [whole(array) for array in others],
-            out_specs=[block, whole(x_own)],
-            scratch_shapes=[pltpu.VMEM((2, cols, NB), jnp.bfloat16)] * 2,
+            out_specs=[block, whole(own), whole(own)],
+            scratch_shapes=[pltpu.VMEM((2, cols, NB), jnp.bfloat16)] * 2
+            + [pltpu.VMEM((NB, NB), jnp.float32)],
         ),
         out_shape=[
             jax.ShapeDtypeStruct((rows, cols), jnp.float32),
-            jax.ShapeDtypeStruct(x_own.shape, jnp.float32),
+            own,
+            own,
         ],
         compiler_params=pltpu.CompilerParams(vmem_limit_bytes=56 * 1024 * 1024),
         cost_estimate=pl.CostEstimate(flops=6_000_000_000, bytes_accessed=16_000_000, transcendentals=0),
         name="update",
-    )(x_index[None], matrix, *others)
+    )(places, matrix, *others)
 
 
 def body(matrix):
@@ -333,13 +342,9 @@
     out_start = col_index * out_rows
     mine = (x_index + XS - out_start // quarter) % XS
 
-    def own(parts):
-        cut = [lax.dynamic_slice_in_dim(part, out_start % quarter, out_rows, 0) for part in parts]
-        return jnp.where(mine < 2, jnp.where(mine == 0, cut[0], cut[1]), jnp.where(mine == 2, cut[2], cut[3]))
-
-    v_own = own(v_parts)
-    updated, w_own = update(
-        x_index, matrix, v_parts, x_parts, v_cols, arrived, inner, t_factor, v_own, own(x_parts)
+    places = jnp.stack([x_index, mine, out_start % quarter])
+    updated, v_own, w_own = update(
+        places, out_rows, matrix, v_parts, x_parts, v_cols, arrived, inner, t_factor
     )
     return (updated, v_own[None], w_own[None])
 

time: 221 us -> 224 us (1.014)
  waiting for transfers between devices: 69.4 us -> 74.5 us
  other arithmetic: 5.61 us -> 3.11 us
    ppermute x9, waiting for transfers between devices: 23.3 us -> 34.8 us  [x_shift(): return lax.ppermute(value, 'col', pairs)]
    all_to_all x9, waiting for transfers between devices: 45.5 us -> 39.1 us  [exchange(): lax.all_to_all(value, axis, 0, 0, tiled=True, axis_index_groups=groups)]
    select_n x2 -> x0, other arithmetic: 3.11 us -> none  [own(): jnp.where(mine < 2, jnp.where(mine == 0, cut[0], cut[1]), jnp.where(mine...]
  transfers between devices with their start and end apart: 20 -> 20, of which waited for: 12 -> 13; matrix products, arithmetic and copies ran while one was open for 11% -> 10% of each run, Pallas kernels for 9% -> 9%
where the time goes in v2:
time: 224 us; the launch traced here: 223 us
  starting transfers between devices  76.3 us (34%)
  waiting for transfers between devices  74.5 us (33%)
  Pallas kernels  30.1 us (13%)
  matrix products  17.6 us (8%)
  blocking collectives  12.5 us (6%)
  local copies, waits for them, and re-layouts  7.48 us (3%)
  other arithmetic  3.11 us (1%)
    all_to_all x9, starting transfers between devices, exchange(): lax.all_to_all(value, axis, 0, 0, tiled=True, axis_index_groups=groups)  50.5 us
    all_to_all x9, waiting for transfers between devices, exchange(): lax.all_to_all(value, axis, 0, 0, tiled=True, axis_index_groups=groups)  39.1 us
    ppermute x9, waiting for transfers between devices, x_shift(): return lax.ppermute(value, 'col', pairs)  34.8 us
    pallas_call x1, Pallas kernels, factor_all(): pl.pallas_call(kernel, out_shape=[sq, sq, sq, sq, sq, jax.ShapeDtypeStruc...  19.1 us
    dot_general x14, matrix products, mm(): lax.dot_general(left, right, (((ca,), (cb,)), ((), ())), precision=precis...  17.6 us
    ppermute x9, starting transfers between devices, x_shift(): return lax.ppermute(value, 'col', pairs)  13.5 us
    all_gather x1, blocking collectives, body(): strip_cols = lax.all_gather(strip_piece, 'row', axis=0, tiled=True)  12.5 us
    ppermute x2, starting transfers between devices, swap(): return lax.ppermute(value, ('row', 'col'), pairs)  12.3 us
  transfers between devices with their start and end apart: 20, of which 13 were waited for; matrix products, arithmetic and copies ran while one was open for 10% of the time, Pallas kernels for 9%

profile of v2, /device:TPU:10, one launch (start us, length us, event | category | flops | bytes accessed | tf_op | source)
XLA Modules:
  0.0 222.5 jit_solution(847511303697502418)
XLA Ops:
  0.6 1.3 slice_bitcast_fusion
  2.5 1.1 pad_maximum_fusion
  3.5 4.9 %all-to-all-start = ((f32[8,128,256]{2,1,0:T(8,128)}), f32[8,128,256]{2,1,0:T(8,128)S(1)}, u32[]{:S(2)}, u32[]{:S(2)}) async-start(f32[8,128,256]{2,1,0:T(8,128)} %pad_maximum_fusion), calls=%async_computation | async-start | bytes 2097152 | tf_op jit(solution)/shard_map/all_to_all | solution.py:173
  8.5 14.5 %all-to-all-done = f32[8,128,256]{2,1,0:T(8,128)S(1)} async-done(((f32[8,128,256]{2,1,0:T(8,128)}), f32[8,128,256]{2,1,0:T(8,128)S(1)}, u32[]{:S(2)}, u32[]{:S(2)}) %all-to-all-start) | async-done | bytes 1048608 | tf_op jit(solution)/shard_map/all_to_all | solution.py:173
  23.0 12.5 %all-gather = f32[1,512,256]{2,1,0:T(8,128)S(1)} all-gather(f32[1,64,256]{2,1,0:T(8,128)S(1)} %slice.55), channel_id=2, replica_groups=mesh['row'=8,'col'=32] {'row'}, dimensions={1}, use_global_device_ids=true | all-gather | bytes 589824 | tf_op jit(solution)/shard_map/all_gather | solution.py:291
  36.9 4.8 %all-to-all-start.1 = ((f32[4,64,256]{2,1,0:T(8,128)}), f32[4,64,256]{2,1,0:T(8,128)S(1)}, u32[]{:S(2)}, u32[]{:S(2)}) async-start(f32[4,64,256]{2,1,0:T(8,128)} %broadcast_in_dim.105), calls=%async_computation.1 | async-start | bytes 524288 | tf_op jit(solution)/shard_map/all_to_all | solution.py:173
  41.7 1.8 fusion.6
  43.5 4.0 %all-to-all-done.1 = f32[4,64,256]{2,1,0:T(8,128)S(1)} async-done(((f32[4,64,256]{2,1,0:T(8,128)}), f32[4,64,256]{2,1,0:T(8,128)S(1)}, u32[]{:S(2)}, u32[]{:S(2)}) %all-to-all-start.1) | async-done | bytes 262176 | tf_op jit(solution)/shard_map/all_to_all | solution.py:173
  47.6 0.9 broadcast_in_dim.106
  48.4 8.4 %all-to-all-start.2 = ((f32[8,64,256]{2,1,0:T(8,128)}), f32[8,64,256]{2,1,0:T(8,128)S(1)}, u32[]{:S(2)}, u32[]{:S(2)}) async-start(f32[8,64,256]{2,1,0:T(8,128)} %broadcast_in_dim.106), calls=%async_computation.2 | async-start | bytes 1048576 | tf_op jit(solution)/shard_map/all_to_all | solution.py:173
  56.8 1.8 fusion.4
  58.6 2.6 %fusion.2 = f32[512,256]{1,0:T(8,128)} fusion(f32[2048,512]{1,0:T(8,128)} %a_ref.1, s32[]{:T(128)S(6)} %select_n.101, f32[1,512,256]{2,1,0:T(8,128)S(1)} %all-gather), kind=kOutput, calls=%fused_computation.9 | convolution fusion | flops 402653184 | bytes 2097156 | tf_op jit(solution)/shard_map/dot_general | solution.py:162
  61.2 1.5 collective-permute-start.2
  63.2 2.7 %collective-permute-start = (f32[512,256]{1,0:T(8,128)S(1)}, f32[512,256]{1,0:T(8,128)}, u32[]{:S(2)}, u32[]{:S(2)}) collective-permute-start(f32[512,256]{1,0:T(8,128)S(1)} %fusion.6), channel_id=1, source_target_pairs={{0,2},{1,3},{2,0},{3,1},{4,6},{5,7},{6,4},{7,5},{8,10},{9,11},{10,... | collective-permute-start | bytes 1572872 | tf_op jit(solution)/shard_map/ppermute | solution.py:182
  65.9 6.3 %collective-permute-start.3 = (f32[128,256]{1,0:T(8,128)S(1)}, f32[128,256]{1,0:T(8,128)S(1)}, u32[]{:S(2)}, u32[]{:S(2)}) collective-permute-start(f32[128,256]{1,0:T(8,128)S(1)} %slice_bitcast_fusion.1), channel_id=1, source_target_pairs={{0,0},{1,1},{2,2},{3,3},{4,32},{5,33},{6,34},{7,35},{8,64},{9,65},... | collective-permute-start | bytes 393224 | tf_op jit(solution)/shard_map/ppermute | solution.py:193
  72.3 1.1 all-to-all-done.2
  73.4 0.9 broadcast_in_dim.107
  74.3 6.7 %all-to-all-start.3 = ((f32[8,64,256]{2,1,0:T(8,128)}), f32[8,64,256]{2,1,0:T(8,128)S(1)}, u32[]{:S(2)}, u32[]{:S(2)}) async-start(f32[8,64,256]{2,1,0:T(8,128)} %broadcast_in_dim.107), calls=%async_computation.3 | async-start | bytes 1048576 | tf_op jit(solution)/shard_map/all_to_all | solution.py:173
  81.6 3.7 %collective-permute-done.2 = f32[512,256]{1,0:T(8,128)} collective-permute-done((f32[512,256]{1,0:T(8,128)}, f32[512,256]{1,0:T(8,128)}, u32[]{:S(2)}, u32[]{:S(2)}) %collective-permute-start.2) | collective-permute-done | bytes 524320 | tf_op jit(solution)/shard_map/ppermute | solution.py:182
  85.2 2.3 %add_add_fusion = f32[512,256]{1,0:T(8,128)S(1)} fusion(f32[512,256]{1,0:T(8,128)} %collective-permute-done.2, f32[512,256]{1,0:T(8,128)} %collective-permute-done, f32[512,256]{1,0:T(8,128)} %collective-permute-done.1, f32[1,512,256]{2,1,0:T(8,128)S(1)} %all-gather, f32[2048,512]{1,0:T(8,128)} %a_ref.1, s32[]{:T(128)S(6)} %select_n.103), kind=kOutput, calls=%fused_computation.25 | convolution fusion | flops 403046400 | bytes 3670020 | tf_op jit(solution)/shard_map/dot_general | solution.py:162
  87.6 1.1 pad_maximum_fusion.1
  88.6 1.2 all-to-all-done.3
  89.9 5.7 %all-to-all-start.4 = ((f32[8,128,256]{2,1,0:T(8,128)}), f32[8,128,256]{2,1,0:T(8,128)S(1)}, u32[]{:S(2)}, u32[]{:S(2)}) async-start(f32[8,128,256]{2,1,0:T(8,128)} %pad_maximum_fusion.1), calls=%async_computation.4 | async-start | bytes 2097152 | tf_op jit(solution)/shard_map/all_to_all | solution.py:173
  95.6 19.1 %factor.1 = (f32[256,256]{1,0:T(8,128)S(1)}, f32[256,256]{1,0:T(8,128)S(1)}, f32[256,256]{1,0:T(8,128)S(1)}, f32[256,256]{1,0:T(8,128)S(1)}, f32[256,256]{1,0:T(8,128)S(1)}, /*index=5*/f32[1,256]{1,0:T(1,128)S(1)}) custom-call(f32[256,256]{1,0:T(8,128)S(1)} %bitcast.53, f32[256,256]{1,0:T(8,128)S(1)} %bitcast.52), custom_call_target="tpu_custom_call" | custom-call | flops 20000000000 | bytes 2000000 | tf_op jit(solution)/shard_map/factor/pallas_call | solution.py:147
  114.7 7.5 %all-to-all-done.4 = f32[8,128,256]{2,1,0:T(8,128)S(1)} async-done(((f32[8,128,256]{2,1,0:T(8,128)}), f32[8,128,256]{2,1,0:T(8,128)S(1)}, u32[]{:S(2)}, u32[]{:S(2)}) %all-to-all-start.4) | async-done | bytes 1048608 | tf_op jit(solution)/shard_map/all_to_all | solution.py:173
  122.9 0.8 broadcast_in_dim.112
  123.8 3.5 %all-to-all-start.5 = ((f32[8,64,256]{2,1,0:T(8,128)}), f32[8,64,256]{2,1,0:T(8,128)S(1)}, u32[]{:S(2)}, u32[]{:S(2)}) async-start(f32[8,64,256]{2,1,0:T(8,128)} %broadcast_in_dim.112), calls=%async_computation.5 | async-start | bytes 1048576 | tf_op jit(solution)/shard_map/all_to_all | solution.py:173
  127.4 6.0 %collective-permute-start.10 = (f32[64,256]{1,0:T(8,128)S(1)}, f32[64,256]{1,0:T(8,128)S(1)}, u32[]{:S(2)}, u32[]{:S(2)}) collective-permute-start(f32[64,256]{1,0:T(8,128)S(1)} %fusion.22), channel_id=1, source_target_pairs={{0,0},{1,1},{2,2},{3,3},{4,32},{5,33},{6,34},{7,35},{8,64},{9,65},... | collective-permute-start | bytes 196616 | tf_op jit(solution)/shard_map/ppermute | solution.py:193
  133.8 8.3 %all-to-all-done.5 = f32[8,64,256]{2,1,0:T(8,128)S(1)} async-done(((f32[8,64,256]{2,1,0:T(8,128)}), f32[8,64,256]{2,1,0:T(8,128)S(1)}, u32[]{:S(2)}, u32[]{:S(2)}) %all-to-all-start.5) | async-done | bytes 524320 | tf_op jit(solution)/shard_map/all_to_all | solution.py:173
  143.3 4.9 %all-to-all-start.6 = ((f32[4,32,256]{2,1,0:T(8,128)}), f32[4,32,256]{2,1,0:T(8,128)S(1)}, u32[]{:S(2)}, u32[]{:S(2)}) async-start(f32[4,32,256]{2,1,0:T(8,128)} %broadcast_in_dim.114), calls=%async_computation.6 | async-start | bytes 262144 | tf_op jit(solution)/shard_map/all_to_all | solution.py:173
  148.8 1.5 collective-permute-start.4
  150.2 2.4 %all-to-all-done.6 = f32[4,32,256]{2,1,0:T(8,128)S(1)} async-done(((f32[4,32,256]{2,1,0:T(8,128)}), f32[4,32,256]{2,1,0:T(8,128)S(1)}, u32[]{:S(2)}, u32[]{:S(2)}) %all-to-all-start.6) | async-done | bytes 131104 | tf_op jit(solution)/shard_map/all_to_all | solution.py:173
  152.7 0.9 broadcast_in_dim.115
  153.7 7.3 %all-to-all-start.7 = ((f32[8,96,256]{2,1,0:T(8,128)}), f32[8,96,256]{2,1,0:T(8,128)S(1)}, u32[]{:S(2)}, u32[]{:S(2)}) async-start(f32[8,96,256]{2,1,0:T(8,128)} %broadcast_in_dim.115), calls=%async_computation.7 | async-start | bytes 1572864 | tf_op jit(solution)/shard_map/all_to_all | solution.py:173
  161.0 1.2 convolution_select_fusion.refs_8_
  162.2 1.5 collective-permute-start.5
  163.6 1.1 fusion.17.refs_11_
  164.7 0.9 collective-permute-start.6
  165.7 2.2 %convolution_select_fusion.3.refs_1_ = f32[512,256]{1,0:T(8,128)} fusion(f32[512,256]{1,0:T(8,128)} %collective-permute-done.4, f32[256,256]{1,0:T(8,128)S(1)} %get-tuple-element.13, f32[256,256]{1,0:T(8,128)S(1)} %get-tuple-element.12, pred[512]{0:T(512)(128)(4,1)S(1)} %fusion.26), kind=kOutput, calls=%fused_computation.3 | convolution fusion | flops 201457664 | bytes 1573376 | tf_op jit(solution)/shard_map/dot_general | solution.py:162
  167.9 2.3 %collective-permute-start.9 = (f32[512,256]{1,0:T(8,128)S(1)}, f32[512,256]{1,0:T(8,128)}, u32[]{:S(2)}, u32[]{:S(2)}) collective-permute-start(f32[512,256]{1,0:T(8,128)S(1)} %bitcast.60), channel_id=1, source_target_pairs={{0,3},{1,0},{2,1},{3,2},{4,7},{5,4},{6,5},{7,6},{8,11},{9,8},{10,9... | collective-permute-start | bytes 1572872 | tf_op jit(solution)/shard_map/ppermute | solution.py:182
  170.5 2.4 %collective-permute-start.7 = (f32[512,256]{1,0:T(8,128)S(1)}, f32[512,256]{1,0:T(8,128)}, u32[]{:S(2)}, u32[]{:S(2)}) collective-permute-start(f32[512,256]{1,0:T(8,128)S(1)} %bitcast.62), channel_id=1, source_target_pairs={{0,1},{1,2},{2,3},{3,0},{4,5},{5,6},{6,7},{7,4},{8,9},{9,10},{10,1... | collective-permute-start | bytes 1572872 | tf_op jit(solution)/shard_map/ppermute | solution.py:182
  173.7 4.3 %all-to-all-start.8 = ((f32[8,32,256]{2,1,0:T(8,128)}), f32[8,32,256]{2,1,0:T(8,128)}, u32[]{:S(2)}, u32[]{:S(2)}) async-start(f32[8,32,256]{2,1,0:T(8,128)} %broadcast_in_dim.116), calls=%async_computation.8 | async-start | bytes 524288 | tf_op jit(solution)/shard_map/all_to_all | solution.py:173
  178.5 1.2 convolution_select_fusion.2.refs_2_
  179.7 9.3 %collective-permute-done.6 = f32[512,256]{1,0:T(8,128)S(1)} collective-permute-done((f32[512,256]{1,0:T(8,128)S(1)}, f32[512,256]{1,0:T(8,128)S(1)}, u32[]{:S(2)}, u32[]{:S(2)}) %collective-permute-start.6) | collective-permute-done | bytes 524320 | tf_op jit(solution)/shard_map/ppermute | solution.py:182
  189.0 1.2 convolution_select_fusion.1.refs_3_
  190.2 10.8 %collective-permute-done.9.refs_7_ = f32[512,256]{1,0:T(8,128)} collective-permute-done((f32[512,256]{1,0:T(8,128)S(1)}, f32[512,256]{1,0:T(8,128)}, u32[]{:S(2)}, u32[]{:S(2)}) %collective-permute-start.9) | collective-permute-done | bytes 524320 | tf_op jit(solution)/shard_map/ppermute | solution.py:182
  201.0 10.5 %collective-permute-done.8.refs_6_ = f32[512,256]{1,0:T(8,128)} collective-permute-done((f32[512,256]{1,0:T(8,128)S(1)}, f32[512,256]{1,0:T(8,128)}, u32[]{:S(2)}, u32[]{:S(2)}) %collective-permute-start.8) | collective-permute-done | bytes 524320 | tf_op jit(solution)/shard_map/ppermute | solution.py:182
  211.5 11.0 %update.1 = (f32[2048,512]{1,0:T(8,128)}, f32[64,256]{1,0:T(8,128)}, f32[64,256]{1,0:T(8,128)}) custom-call(s32[3]{0:T(128)} %pad_add_fusion.at, f32[2048,512]{1,0:T(8,128)} %a_ref.1, f32[512,256]{1,0:T(8,128)} %copy-done.2, f32[512,256]{1,0:T(8,128)} %convolution_select_fusion.3.refs_1_, f32[512,256]{1,0:T(8,128)} %convolution_select_fusion.2.refs_2_, ...), custom_call_target="tpu_custom_call" | custom-call | flops 6000000000 | bytes 16000000 | tf_op jit(solution)/shard_map/update/pallas_call | solution.py:253
  (48 shorter events, 7.7 us)
Async XLA Ops:
  3.5 19.4 %all-to-all-start = ((f32[8,128,256]{2,1,0:T(8,128)}), f32[8,128,256]{2,1,0:T(8,128)S(1)}, u32[]{:S(2)}, u32[]{:S(2)}) async-start(f32[8,128,256]{2,1,0:T(8,128)} %pad_maximum_fusion), calls=%async_computation | async-start | bytes 2097152 | tf_op jit(solution)/shard_map/all_to_all | solution.py:173
  36.9 10.7 %all-to-all-start.1 = ((f32[4,64,256]{2,1,0:T(8,128)}), f32[4,64,256]{2,1,0:T(8,128)S(1)}, u32[]{:S(2)}, u32[]{:S(2)}) async-start(f32[4,64,256]{2,1,0:T(8,128)} %broadcast_in_dim.105), calls=%async_computation.1 | async-start | bytes 524288 | tf_op jit(solution)/shard_map/all_to_all | solution.py:173
  48.4 25.0 %all-to-all-start.2 = ((f32[8,64,256]{2,1,0:T(8,128)}), f32[8,64,256]{2,1,0:T(8,128)S(1)}, u32[]{:S(2)}, u32[]{:S(2)}) async-start(f32[8,64,256]{2,1,0:T(8,128)} %broadcast_in_dim.106), calls=%async_computation.2 | async-start | bytes 1048576 | tf_op jit(solution)/shard_map/all_to_all | solution.py:173
  61.2 24.0 %collective-permute-start.2 = (f32[512,256]{1,0:T(8,128)}, f32[512,256]{1,0:T(8,128)}, u32[]{:S(2)}, u32[]{:S(2)}) collective-permute-start(f32[512,256]{1,0:T(8,128)} %fusion.2), channel_id=1, source_target_pairs={{0,3},{1,0},{2,1},{3,2},{4,7},{5,4},{6,5},{7,6},{8,11},{9,8},{10,9... | collective-permute-start | bytes 1572872 | tf_op jit(solution)/shard_map/ppermute | solution.py:182
  62.7 22.6 %collective-permute-start.1 = (f32[512,256]{1,0:T(8,128)S(1)}, f32[512,256]{1,0:T(8,128)}, u32[]{:S(2)}, u32[]{:S(2)}) collective-permute-start(f32[512,256]{1,0:T(8,128)S(1)} %fusion.4), channel_id=1, source_target_pairs={{0,1},{1,2},{2,3},{3,0},{4,5},{5,6},{6,7},{7,4},{8,9},{9,10},{10,1... | collective-permute-start | bytes 1572872 | tf_op jit(solution)/shard_map/ppermute | solution.py:182
  63.2 22.0 %collective-permute-start = (f32[512,256]{1,0:T(8,128)S(1)}, f32[512,256]{1,0:T(8,128)}, u32[]{:S(2)}, u32[]{:S(2)}) collective-permute-start(f32[512,256]{1,0:T(8,128)S(1)} %fusion.6), channel_id=1, source_target_pairs={{0,2},{1,3},{2,0},{3,1},{4,6},{5,7},{6,4},{7,5},{8,10},{9,11},{10,... | collective-permute-start | bytes 1572872 | tf_op jit(solution)/shard_map/ppermute | solution.py:182
  65.9 15.7 %collective-permute-start.3 = (f32[128,256]{1,0:T(8,128)S(1)}, f32[128,256]{1,0:T(8,128)S(1)}, u32[]{:S(2)}, u32[]{:S(2)}) collective-permute-start(f32[128,256]{1,0:T(8,128)S(1)} %slice_bitcast_fusion.1), channel_id=1, source_target_pairs={{0,0},{1,1},{2,2},{3,3},{4,32},{5,33},{6,34},{7,35},{8,64},{9,65},... | collective-permute-start | bytes 393224 | tf_op jit(solution)/shard_map/ppermute | solution.py:193
  74.3 15.6 %all-to-all-start.3 = ((f32[8,64,256]{2,1,0:T(8,128)}), f32[8,64,256]{2,1,0:T(8,128)S(1)}, u32[]{:S(2)}, u32[]{:S(2)}) async-start(f32[8,64,256]{2,1,0:T(8,128)} %broadcast_in_dim.107), calls=%async_computation.3 | async-start | bytes 1048576 | tf_op jit(solution)/shard_map/all_to_all | solution.py:173
  89.9 32.3 %all-to-all-start.4 = ((f32[8,128,256]{2,1,0:T(8,128)}), f32[8,128,256]{2,1,0:T(8,128)S(1)}, u32[]{:S(2)}, u32[]{:S(2)}) async-start(f32[8,128,256]{2,1,0:T(8,128)} %pad_maximum_fusion.1), calls=%async_computation.4 | async-start | bytes 2097152 | tf_op jit(solution)/shard_map/all_to_all | solution.py:173
  123.8 18.3 %all-to-all-start.5 = ((f32[8,64,256]{2,1,0:T(8,128)}), f32[8,64,256]{2,1,0:T(8,128)S(1)}, u32[]{:S(2)}, u32[]{:S(2)}) async-start(f32[8,64,256]{2,1,0:T(8,128)} %broadcast_in_dim.112), calls=%async_computation.5 | async-start | bytes 1048576 | tf_op jit(solution)/shard_map/all_to_all | solution.py:173
  127.4 25.3 %collective-permute-start.10 = (f32[64,256]{1,0:T(8,128)S(1)}, f32[64,256]{1,0:T(8,128)S(1)}, u32[]{:S(2)}, u32[]{:S(2)}) collective-permute-start(f32[64,256]{1,0:T(8,128)S(1)} %fusion.22), channel_id=1, source_target_pairs={{0,0},{1,1},{2,2},{3,3},{4,32},{5,33},{6,34},{7,35},{8,64},{9,65},... | collective-permute-start | bytes 196616 | tf_op jit(solution)/shard_map/ppermute | solution.py:193
  133.8 19.9 %copy-start.2 = (f32[512,256]{1,0:T(8,128)}, f32[512,256]{1,0:T(8,128)S(1)}, u32[]{:S(2)}) copy-start(f32[512,256]{1,0:T(8,128)S(1)} %convolution_select_fusion.4.refs_0_) | copy-start | bytes 1572868
  142.1 31.6 %copy-start = (f32[8,64,256]{2,1,0:T(8,128)}, f32[8,64,256]{2,1,0:T(8,128)S(1)}, u32[]{:S(2)}) copy-start(f32[8,64,256]{2,1,0:T(8,128)S(1)} %all-to-all-done.5) | copy-start | bytes 1572868
  143.3 9.4 %all-to-all-start.6 = ((f32[4,32,256]{2,1,0:T(8,128)}), f32[4,32,256]{2,1,0:T(8,128)S(1)}, u32[]{:S(2)}, u32[]{:S(2)}) async-start(f32[4,32,256]{2,1,0:T(8,128)} %broadcast_in_dim.114), calls=%async_computation.6 | async-start | bytes 262144 | tf_op jit(solution)/shard_map/all_to_all | solution.py:173
  148.8 16.9 %collective-permute-start.4 = (f32[512,256]{1,0:T(8,128)S(1)}, f32[512,256]{1,0:T(8,128)}, u32[]{:S(2)}, u32[]{:S(2)}) collective-permute-start(f32[512,256]{1,0:T(8,128)S(1)} %bitcast.56), channel_id=1, source_target_pairs={{0,1},{1,2},{2,3},{3,0},{4,5},{5,6},{6,7},{7,4},{8,9},{9,10},{10,1... | collective-permute-start | bytes 1572872 | tf_op jit(solution)/shard_map/ppermute | solution.py:182
  153.7 19.2 %all-to-all-start.7 = ((f32[8,96,256]{2,1,0:T(8,128)}), f32[8,96,256]{2,1,0:T(8,128)S(1)}, u32[]{:S(2)}, u32[]{:S(2)}) async-start(f32[8,96,256]{2,1,0:T(8,128)} %broadcast_in_dim.115), calls=%async_computation.7 | async-start | bytes 1572864 | tf_op jit(solution)/shard_map/all_to_all | solution.py:173
  162.2 16.3 %collective-permute-start.5 = (f32[512,256]{1,0:T(8,128)S(1)}, f32[512,256]{1,0:T(8,128)S(1)}, u32[]{:S(2)}, u32[]{:S(2)}) collective-permute-start(f32[512,256]{1,0:T(8,128)S(1)} %bitcast.57), channel_id=1, source_target_pairs={{0,2},{1,3},{2,0},{3,1},{4,6},{5,7},{6,4},{7,5},{8,10},{9,11},{10,... | collective-permute-start | bytes 1572872 | tf_op jit(solution)/shard_map/ppermute | solution.py:182
  164.7 24.2 %collective-permute-start.6 = (f32[512,256]{1,0:T(8,128)S(1)}, f32[512,256]{1,0:T(8,128)S(1)}, u32[]{:S(2)}, u32[]{:S(2)}) collective-permute-start(f32[512,256]{1,0:T(8,128)S(1)} %bitcast.58), channel_id=1, source_target_pairs={{0,3},{1,0},{2,1},{3,2},{4,7},{5,4},{6,5},{7,6},{8,11},{9,8},{10,9... | collective-permute-start | bytes 1572872 | tf_op jit(solution)/shard_map/ppermute | solution.py:182
  167.9 33.1 %collective-permute-start.9 = (f32[512,256]{1,0:T(8,128)S(1)}, f32[512,256]{1,0:T(8,128)}, u32[]{:S(2)}, u32[]{:S(2)}) collective-permute-start(f32[512,256]{1,0:T(8,128)S(1)} %bitcast.60), channel_id=1, source_target_pairs={{0,3},{1,0},{2,1},{3,2},{4,7},{5,4},{6,5},{7,6},{8,11},{9,8},{10,9... | collective-permute-start | bytes 1572872 | tf_op jit(solution)/shard_map/ppermute | solution.py:182
  170.2 41.3 %collective-permute-start.8 = (f32[512,256]{1,0:T(8,128)S(1)}, f32[512,256]{1,0:T(8,128)}, u32[]{:S(2)}, u32[]{:S(2)}) collective-permute-start(f32[512,256]{1,0:T(8,128)S(1)} %bitcast.61), channel_id=1, source_target_pairs={{0,2},{1,3},{2,0},{3,1},{4,6},{5,7},{6,4},{7,5},{8,10},{9,11},{10,... | collective-permute-start | bytes 1572872 | tf_op jit(solution)/shard_map/ppermute | solution.py:182
  170.5 41.0 %collective-permute-start.7 = (f32[512,256]{1,0:T(8,128)S(1)}, f32[512,256]{1,0:T(8,128)}, u32[]{:S(2)}, u32[]{:S(2)}) collective-permute-start(f32[512,256]{1,0:T(8,128)S(1)} %bitcast.62), channel_id=1, source_target_pairs={{0,1},{1,2},{2,3},{3,0},{4,5},{5,6},{6,7},{7,4},{8,9},{9,10},{10,1... | collective-permute-start | bytes 1572872 | tf_op jit(solution)/shard_map/ppermute | solution.py:182
  172.9 38.7 %copy-start.1 = (f32[8,96,256]{2,1,0:T(8,128)}, f32[8,96,256]{2,1,0:T(8,128)S(1)}, u32[]{:S(2)}) copy-start(f32[8,96,256]{2,1,0:T(8,128)S(1)} %all-to-all-done.7.refs_9_) | copy-start | bytes 2359300
  173.7 37.8 %all-to-all-start.8 = ((f32[8,32,256]{2,1,0:T(8,128)}), f32[8,32,256]{2,1,0:T(8,128)}, u32[]{:S(2)}, u32[]{:S(2)}) async-start(f32[8,32,256]{2,1,0:T(8,128)} %broadcast_in_dim.116), calls=%async_computation.8 | async-start | bytes 524288 | tf_op jit(solution)/shard_map/all_to_all | solution.py:173
